TPU v7x, 128 devices: a whole 4x4x4 slice. The times are simulated.
128 devices in a mesh: lat: 16 (over z, x_lo, core), lon: 4 (over y), batch: 2 (over x_hi).
Axes of the slice: x: 4 (x_hi: 2, x_lo: 2; x = x_hi * 2 + x_lo), y: 4, z: 4, core: 2. Of those that a mesh axis runs over, the one named last changes fastest.
Arguments:
- inputs: bfloat16 [4, 128, 360, 1024], P('batch', 'lat', 'lon'), may hold values from -6 to 6
- cotangent: bfloat16 [4, 128, 360, 1024], P('batch', 'lat', 'lon'), may hold values from -6 to 6
- area_weight: float32 [128], P('lat'), may hold values from 0.2 to 2
- first_weight: bfloat16 [2, 8, 128, 128], P(None, 'lon'), may hold values from -0.375 to 0.375
- first_bias: bfloat16 [2, 8, 128], P(None, 'lon'), may hold values from -0.59765625 to 0.59765625
- second_weight: bfloat16 [2, 8, 128, 128], P(None, 'lon'), may hold values from -0.375 to 0.375
- second_bias: bfloat16 [2, 8, 128], P(None, 'lon'), may hold values from -0.59765625 to 0.59765625
Outputs:
- output_field: bfloat16 [4, 128, 360, 1024], P('batch', 'lat', 'lon')
- grad_input: bfloat16 [4, 128, 360, 1024], P('batch', 'lat', 'lon')
- grad_first_weight: float32 [2, 8, 128, 128], P(None, 'lon')
- grad_second_weight: float32 [2, 8, 128, 128], P(None, 'lon')
- grad_first_bias: float32 [2, 8, 128], P(None, 'lon')
- grad_second_bias: float32 [2, 8, 128], P(None, 'lon')
All inputs are finite; a program needn't handle non-finite values.
Results may differ from a plain program's by a relative error of at most 0.033.
Values may be sent and summed in bfloat16 or wider, within the bound.
A program may use at most 128 MiB of HBM per device.

v0:
```python
import math

import jax
import jax.numpy as jnp
from jax import lax
from jax.sharding import PartitionSpec as P

MODES = 176


shrink_level = 0.25


def contract(pattern, left, right):
    return jnp.einsum(pattern, left, right, preferred_element_type=jnp.float32)


def lon_tables(length, modes_kept):
    column_index = jnp.arange(length, dtype=jnp.int32)[:, None]
    mode_index = jnp.arange(modes_kept, dtype=jnp.int32)[None, :]
    phase_angle = (column_index * mode_index % length).astype(jnp.float32) * (
        2.0 * math.pi / length
    )
    scale_factor = 1.0 / math.sqrt(length)
    cosine = jnp.cos(phase_angle) * scale_factor
    sine = jnp.sin(phase_angle) * scale_factor
    forward_table = jnp.stack([cosine, -sine], axis=1)
    mode_weight = jnp.where(mode_index == 0, 1.0, 2.0).astype(jnp.float32)
    inverse_table = jnp.stack([(mode_weight * cosine).T, (-mode_weight * sine).T], axis=0)
    return (forward_table.astype(jnp.bfloat16), inverse_table.astype(jnp.bfloat16))


def lat_table(length):
    row_index = jnp.arange(length, dtype=jnp.int32)
    phase_angle = (row_index[:, None] * row_index[None, :] % length).astype(jnp.float32) * (
        2.0 * math.pi / length
    )
    scale_factor = 1.0 / math.sqrt(length)
    cosine = jnp.cos(phase_angle) * scale_factor
    sine = jnp.sin(phase_angle) * scale_factor
    upper = jnp.stack([cosine, -sine], axis=1)
    lower = jnp.stack([sine, cosine], axis=1)
    return jnp.stack([upper, lower], axis=0).astype(jnp.bfloat16)


def spectral_forward(spectrum, first_weight, first_bias, second_weight, second_bias):
    members, lat_modes, parts, lon_modes, channels = spectrum.shape
    block_count = first_weight.shape[1]
    block_width = first_weight.shape[2]
    blocks = spectrum.reshape(members, lat_modes, parts, lon_modes, block_count, block_width)
    real_in = blocks[:, :, 0]
    imag_in = blocks[:, :, 1]
    pattern = "bmknd,nde->bmkne"
    pre_real = (
        contract(pattern, real_in, first_weight[0])
        - contract(pattern, imag_in, first_weight[1])
        + first_bias[0].astype(jnp.float32)
    )
    pre_imag = (
        contract(pattern, imag_in, first_weight[0])
        + contract(pattern, real_in, first_weight[1])
        + first_bias[1].astype(jnp.float32)
    )
    hid_real = jax.nn.gelu(pre_real).astype(jnp.bfloat16)
    hid_imag = jax.nn.gelu(pre_imag).astype(jnp.bfloat16)
    out_real = (
        contract(pattern, hid_real, second_weight[0])
        - contract(pattern, hid_imag, second_weight[1])
        + second_bias[0].astype(jnp.float32)
    )
    out_imag = (
        contract(pattern, hid_imag, second_weight[0])
        + contract(pattern, hid_real, second_weight[1])
        + second_bias[1].astype(jnp.float32)
    )
    shrunk_real = out_real - shrink_level * jnp.tanh(out_real / shrink_level)
    shrunk_imag = out_imag - shrink_level * jnp.tanh(out_imag / shrink_level)
    shrunk = (
        jnp.stack([shrunk_real, shrunk_imag], axis=2)
        .reshape(members, lat_modes, parts, lon_modes, channels)
        .astype(jnp.bfloat16)
    )
    saved = (real_in, imag_in, pre_real, pre_imag, hid_real, hid_imag, out_real, out_imag)
    return (shrunk, saved)


def spectral_backward(grad_shrunk, saved, first_weight, second_weight):
    real_in, imag_in, pre_real, pre_imag, hid_real, hid_imag, out_real, out_imag = saved
    members, lat_modes, parts, lon_modes, channels = grad_shrunk.shape
    blocks = grad_shrunk.reshape(
        members, lat_modes, parts, lon_modes, real_in.shape[3], real_in.shape[4]
    )
    slope_real = jnp.tanh(out_real / shrink_level)
    slope_imag = jnp.tanh(out_imag / shrink_level)
    dout_real = (blocks[:, :, 0].astype(jnp.float32) * slope_real * slope_real).astype(jnp.bfloat16)
    dout_imag = (blocks[:, :, 1].astype(jnp.float32) * slope_imag * slope_imag).astype(jnp.bfloat16)
    over_rows = "bmknd,bmkne->nde"
    backward = "bmkne,nde->bmknd"
    gw2_real = contract(over_rows, hid_real, dout_real) + contract(over_rows, hid_imag, dout_imag)
    gw2_imag = contract(over_rows, hid_real, dout_imag) - contract(over_rows, hid_imag, dout_real)
    gb2 = jnp.stack(
        [
            jnp.sum(dout_real.astype(jnp.float32), axis=(0, 1, 2)),
            jnp.sum(dout_imag.astype(jnp.float32), axis=(0, 1, 2)),
        ],
        axis=0,
    )
    dhid_real = contract(backward, dout_real, second_weight[0]) + contract(
        backward, dout_imag, second_weight[1]
    )
    dhid_imag = contract(backward, dout_imag, second_weight[0]) - contract(
        backward, dout_real, second_weight[1]
    )
    dpre_real = jax.vjp(jax.nn.gelu, pre_real)[1](dhid_real)[0].astype(jnp.bfloat16)
    dpre_imag = jax.vjp(jax.nn.gelu, pre_imag)[1](dhid_imag)[0].astype(jnp.bfloat16)
    gw1_real = contract(over_rows, real_in, dpre_real) + contract(over_rows, imag_in, dpre_imag)
    gw1_imag = contract(over_rows, real_in, dpre_imag) - contract(over_rows, imag_in, dpre_real)
    gb1 = jnp.stack(
        [
            jnp.sum(dpre_real.astype(jnp.float32), axis=(0, 1, 2)),
            jnp.sum(dpre_imag.astype(jnp.float32), axis=(0, 1, 2)),
        ],
        axis=0,
    )
    dspec_real = contract(backward, dpre_real, first_weight[0]) + contract(
        backward, dpre_imag, first_weight[1]
    )
    dspec_imag = contract(backward, dpre_imag, first_weight[0]) - contract(
        backward, dpre_real, first_weight[1]
    )
    grad_spectrum = (
        jnp.stack([dspec_real, dspec_imag], axis=2)
        .reshape(members, lat_modes, parts, lon_modes, channels)
        .astype(jnp.bfloat16)
    )
    grad_terms = (
        jnp.stack([gw1_real, gw1_imag], axis=0),
        jnp.stack([gw2_real, gw2_imag], axis=0),
        gb1,
        gb2,
    )
    return (grad_spectrum, grad_terms)


def per_device(
    inputs, cotangent, area_weight, first_weight, first_bias, second_weight, second_bias
):
    members_here, rows_here, cols_here, channels = inputs.shape
    width_total = cols_here * lax.axis_size("lon")
    height_total = rows_here * lax.axis_size("lat")
    members_total = members_here * lax.axis_size("batch")
    lon_forward_table, lon_inverse_table = lon_tables(width_total, MODES)
    lat_square = lat_table(height_total)
    weighted = (area_weight[None, :, None, None] * cotangent.astype(jnp.float32)).astype(
        jnp.bfloat16
    )

    def along_lat(modes_block):
        return contract("bhpkc,phqm->bmqkc", modes_block, lat_square).astype(jnp.bfloat16)

    def back_lat(modes_block):
        return contract("bmqkc,phqm->bhpkc", modes_block, lat_square).astype(jnp.bfloat16)

    half_modes = contract(
        "bhwc,wpk->bhpkc",
        lax.all_to_all(inputs, "lon", split_axis=3, concat_axis=2, tiled=True),
        lon_forward_table,
    ).astype(jnp.bfloat16)
    spectrum = along_lat(lax.all_to_all(half_modes, "lat", split_axis=3, concat_axis=1, tiled=True))
    shrunk, saved = spectral_forward(spectrum, first_weight, first_bias, second_weight, second_bias)
    spatial = back_lat(shrunk)
    pencil_out = contract(
        "bhpkc,pkw->bhwc",
        lax.all_to_all(spatial, "lat", split_axis=1, concat_axis=3, tiled=True),
        lon_inverse_table,
    ).astype(jnp.bfloat16)
    correction = lax.all_to_all(pencil_out, "lon", split_axis=2, concat_axis=3, tiled=True)
    cot_modes = contract(
        "bhwc,pkw->bhpkc",
        lax.all_to_all(weighted, "lon", split_axis=3, concat_axis=2, tiled=True),
        lon_inverse_table,
    ).astype(jnp.bfloat16)
    cot_spectrum = along_lat(
        lax.all_to_all(cot_modes, "lat", split_axis=3, concat_axis=1, tiled=True)
    )
    grad_spectrum, grad_terms = spectral_backward(cot_spectrum, saved, first_weight, second_weight)
    grad_spatial = back_lat(grad_spectrum)
    pencil_grad = contract(
        "bhpkc,wpk->bhwc",
        lax.all_to_all(grad_spatial, "lat", split_axis=1, concat_axis=3, tiled=True),
        lon_forward_table,
    ).astype(jnp.bfloat16)
    grad_tokens = lax.all_to_all(pencil_grad, "lon", split_axis=2, concat_axis=3, tiled=True)
    output_field = (inputs.astype(jnp.float32) + correction.astype(jnp.float32)).astype(
        jnp.bfloat16
    )
    grad_input = (weighted.astype(jnp.float32) + grad_tokens.astype(jnp.float32)).astype(
        jnp.bfloat16
    )
    first_local, second_local, first_bias_local, second_bias_local = grad_terms
    totals = (
        lax.psum(first_local.astype(jnp.bfloat16), ("lat", "batch")).astype(jnp.float32),
        lax.psum(second_local.astype(jnp.bfloat16), ("lat", "batch")).astype(jnp.float32),
        lax.psum(first_bias_local.astype(jnp.bfloat16), ("lat", "batch")).astype(jnp.float32),
        lax.psum(second_bias_local.astype(jnp.bfloat16), ("lat", "batch")).astype(jnp.float32),
    )
    factor = 1.0 / math.sqrt(members_total * height_total * MODES)
    return (
        output_field,
        grad_input,
        totals[0] * factor,
        totals[1] * factor,
        totals[2] * factor,
        totals[3] * factor,
    )


def solution(mesh):
    return jax.shard_map(
        per_device,
        mesh=mesh,
        in_specs=(
            P("batch", "lat", "lon", None),
            P("batch", "lat", "lon", None),
            P("lat"),
            P(None, "lon", None, None),
            P(None, "lon", None),
            P(None, "lon", None, None),
            P(None, "lon", None),
        ),
        out_specs=(
            P("batch", "lat", "lon", None),
            P("batch", "lat", "lon", None),
            P(None, "lon", None, None),
            P(None, "lon", None, None),
            P(None, "lon", None),
            P(None, "lon", None),
        ),
        check_vma=False,
    )
```

profile of v0, /device:TPU:1, one launch (start us, length us, event | category | flops | bytes accessed | tf_op | source)
XLA Modules:
  0.0 507.9 jit_solution(6368926016501614407)
XLA Ops:
  7.2 7.1 %copy.293 = bf16[2,8,90,1024]{2,1,0,3:T(8,128)(2,1)} copy(bf16[2,8,90,1024]{3,1,2,0:T(8,128)(2,1)} %param.7) | data formatting | bytes 5898240 | tf_op args[0]
  14.2 5.1 %all-to-all-start = ((bf16[2,8,90,1024]{2,1,0,3:T(8,128)(2,1)}), bf16[2,8,90,1024]{2,1,0,3:T(8,128)(2,1)}, u32[]{:S(2)}, u32[]{:S(2)}) async-start(bf16[2,8,90,1024]{2,1,0,3:T(8,128)(2,1)} %copy.293), calls=%async_computation | async-start | bytes 8388608 | tf_op jit(solution)/shard_map/all_to_all | solution.py:166
  19.4 3.0 multiply_convert_fusion
  22.3 5.6 %copy.316 = bf16[2,8,90,1024]{2,1,0,3:T(8,128)(2,1)} copy(bf16[2,8,90,1024]{3,1,2,0:T(8,128)(2,1)S(1)} %multiply_convert_fusion) | data formatting | bytes 5898240 | tf_op jit(solution)/shard_map/convert_element_type | solution.py:154
  28.0 40.3 %all-to-all-done = bf16[2,8,90,1024]{2,1,0,3:T(8,128)(2,1)} async-done(((bf16[2,8,90,1024]{2,1,0,3:T(8,128)(2,1)}), bf16[2,8,90,1024]{2,1,0,3:T(8,128)(2,1)}, u32[]{:S(2)}, u32[]{:S(2)}) %all-to-all-start) | async-done | bytes 2949152 | tf_op jit(solution)/shard_map/all_to_all | solution.py:166
  68.2 4.9 all-to-all-start.4
  74.4 8.1 %copy.409 = bf16[2,8,90,4,256]{4,3,1,2,0:T(4,128)(2,1)S(1)} copy(bf16[2,8,90,4,256]{2,1,0,4,3:T(8,128)(2,1)} %bitcast.10) | data formatting | bytes 5898240 | tf_op jit(solution)/shard_map/all_to_all | solution.py:166
  87.1 33.3 %all-to-all-done.4 = bf16[2,8,90,1024]{2,1,0,3:T(8,128)(2,1)} async-done(((bf16[2,8,90,1024]{2,1,0,3:T(8,128)(2,1)}), bf16[2,8,90,1024]{2,1,0,3:T(8,128)(2,1)}, u32[]{:S(2)}, u32[]{:S(2)}) %all-to-all-start.4) | async-done | bytes 2949152 | tf_op jit(solution)/shard_map/all_to_all | solution.py:180
  120.5 9.2 %all-to-all-start.1 = ((bf16[2,8,2,176,256]{4,1,0,2,3:T(8,128)(2,1)}), bf16[2,8,2,176,256]{4,1,0,2,3:T(8,128)(2,1)}, u32[]{:S(2)}, u32[]{:S(2)}) async-start(bf16[2,8,2,176,256]{4,1,0,2,3:T(8,128)(2,1)} %copy.297), calls=%async_computation.1 | async-start | bytes 5767168 | tf_op jit(solution)/shard_map/all_to_all | solution.py:169
  130.9 8.1 %copy.413 = bf16[2,8,90,4,256]{4,3,1,2,0:T(4,128)(2,1)S(1)} copy(bf16[2,8,90,4,256]{2,1,0,4,3:T(8,128)(2,1)} %bitcast.71) | data formatting | bytes 5898240 | tf_op jit(solution)/shard_map/all_to_all | solution.py:180
  143.6 21.5 %all-to-all-done.1 = bf16[2,8,2,176,256]{4,1,0,2,3:T(8,128)(2,1)} async-done(((bf16[2,8,2,176,256]{4,1,0,2,3:T(8,128)(2,1)}), bf16[2,8,2,176,256]{4,1,0,2,3:T(8,128)(2,1)}, u32[]{:S(2)}, u32[]{:S(2)}) %all-to-all-start.1) | async-done | bytes 2883616 | tf_op jit(solution)/shard_map/all_to_all | solution.py:169
  165.1 4.7 all-to-all-start.5
  171.5 4.3 fusion.24
  175.9 6.4 %reshape.315 = bf16[2,128,2,11,2,128]{5,4,1,3,0,2:T(2,128)(2,1)} reshape(bf16[2,128,2,11,256]{4,1,3,0,2:T(8,128)(2,1)} %fusion.24) | data formatting | bytes 5767168 | tf_op jit(solution)/shard_map/reshape | solution.py:50
  182.3 4.5 fusion.278
  191.4 13.9 %all-to-all-done.5 = bf16[2,8,2,176,256]{4,1,0,2,3:T(8,128)(2,1)S(1)} async-done(((bf16[2,8,2,176,256]{4,1,0,2,3:T(8,128)(2,1)}), bf16[2,8,2,176,256]{4,1,0,2,3:T(8,128)(2,1)S(1)}, u32[]{:S(2)}, u32[]{:S(2)}) %all-to-all-start.5) | async-done | bytes 2883616 | tf_op jit(solution)/shard_map/all_to_all | solution.py:184
  207.8 3.4 copy.323
  228.5 3.1 fusion.280
  232.1 3.1 fusion.279
  246.5 4.5 copy.339
  251.1 4.4 all-to-all-start.6
  265.8 2.7 fusion.25
  268.5 4.5 copy.309
  273.1 18.0 %all-to-all-done.6 = bf16[2,128,2,11,256]{4,2,3,0,1:T(2,128)(2,1)S(1)} async-done(((bf16[2,128,2,11,256]{4,2,3,0,1:T(2,128)(2,1)}), bf16[2,128,2,11,256]{4,2,3,0,1:T(2,128)(2,1)S(1)}, u32[]{:S(2)}, u32[]{:S(2)}) %all-to-all-start.6) | async-done | bytes 2883616 | tf_op jit(solution)/shard_map/all_to_all | solution.py:190
  292.7 4.7 all-to-all-start.2
  297.3 3.3 fusion.100
  306.0 26.8 %all-to-all-done.2 = bf16[2,128,2,11,256]{4,2,3,0,1:T(2,128)(2,1)S(1)} async-done(((bf16[2,128,2,11,256]{4,2,3,0,1:T(2,128)(2,1)}), bf16[2,128,2,11,256]{4,2,3,0,1:T(2,128)(2,1)S(1)}, u32[]{:S(2)}, u32[]{:S(2)}) %all-to-all-start.2) | async-done | bytes 2883616 | tf_op jit(solution)/shard_map/all_to_all | solution.py:174
  334.4 3.7 all-to-all-start.7
  352.6 20.1 %all-to-all-done.7 = bf16[2,8,360,256]{3,1,0,2:T(8,128)(2,1)S(1)} async-done(((bf16[2,8,360,256]{3,1,0,2:T(8,128)(2,1)}), bf16[2,8,360,256]{3,1,0,2:T(8,128)(2,1)S(1)}, u32[]{:S(2)}, u32[]{:S(2)}) %all-to-all-start.7) | async-done | bytes 2949152 | tf_op jit(solution)/shard_map/all_to_all | solution.py:193
  372.7 4.6 all-to-all-start.3
  378.2 65.8 %all-reduce = (bf16[2,2,128]{2,1,0:T(2,128)(2,1)S(1)}, bf16[2,2,128]{2,1,0:T(2,128)(2,1)S(1)}) all-reduce(bf16[2,2,128]{2,1,0:T(2,128)(2,1)S(1)} %pad_maximum_fusion.11, bf16[2,2,128]{2,1,0:T(2,128)(2,1)S(1)} %pad_maximum_fusion.12), channel_id=1, replica_groups=mesh['lat'=16,'lon'=4,'batch'=2] {'lat','batch'}, use_global_device_ids=true, to_apply=%region_4.5 | all-reduce | flops 1024 | bytes 4096 | tf_op jit(solution)/shard_map/psum | solution.py:204
  445.1 40.0 %all-reduce.4.cloned.1.call-done = (bf16[2,2,128,128]{3,2,1,0:T(8,128)(2,1)}, bf16[2,2,128,128]{3,2,1,0:T(8,128)(2,1)}) async-done(((bf16[2,2,128,128]{3,2,1,0:T(8,128)(2,1)}, bf16[2,2,128,128]{3,2,1,0:T(8,128)(2,1)}), (bf16[2,2,128,128]{3,2,1,0:T(8,128)(2,1)}, bf16[2,2,128,128]{3,2,1,0:T(8,128)(2,1)})) %all-reduce.4.cloned.1.call-update) | async-done | bytes 262160 | tf_op jit(solution)/shard_map/psum | solution.py:202
  (158 shorter events, 100.2 us)
Async XLA Ops:
  14.2 5.1 %copy-start.31 = (f32[8]{0:T(128)S(1)}, f32[8]{0:T(128)}, u32[]{:S(2)}) copy-start(f32[8]{0:T(128)} %param.9) | copy-start | bytes 100
  14.2 54.0 %all-to-all-start = ((bf16[2,8,90,1024]{2,1,0,3:T(8,128)(2,1)}), bf16[2,8,90,1024]{2,1,0,3:T(8,128)(2,1)}, u32[]{:S(2)}, u32[]{:S(2)}) async-start(bf16[2,8,90,1024]{2,1,0,3:T(8,128)(2,1)} %copy.293), calls=%async_computation | async-start | bytes 8388608 | tf_op jit(solution)/shard_map/all_to_all | solution.py:166
  68.2 52.2 %all-to-all-start.4 = ((bf16[2,8,90,1024]{2,1,0,3:T(8,128)(2,1)}), bf16[2,8,90,1024]{2,1,0,3:T(8,128)(2,1)}, u32[]{:S(2)}, u32[]{:S(2)}) async-start(bf16[2,8,90,1024]{2,1,0,3:T(8,128)(2,1)} %copy.316), calls=%async_computation.4 | async-start | bytes 8388608 | tf_op jit(solution)/shard_map/all_to_all | solution.py:180
  74.4 8.5 %copy-start.28 = (bf16[360,1,176]{0,2,1:T(8,128)(2,1)}, bf16[360,1,176]{0,2,1:T(8,128)(2,1)S(1)}, u32[]{:S(2)}) copy-start(bf16[360,1,176]{0,2,1:T(8,128)(2,1)S(1)} %get-tuple-element.37) | copy-start | bytes 380164
  120.5 44.6 %all-to-all-start.1 = ((bf16[2,8,2,176,256]{4,1,0,2,3:T(8,128)(2,1)}), bf16[2,8,2,176,256]{4,1,0,2,3:T(8,128)(2,1)}, u32[]{:S(2)}, u32[]{:S(2)}) async-start(bf16[2,8,2,176,256]{4,1,0,2,3:T(8,128)(2,1)} %copy.297), calls=%async_computation.1 | async-start | bytes 5767168 | tf_op jit(solution)/shard_map/all_to_all | solution.py:169
  143.6 26.8 %copy-start.34 = (bf16[2,2,128]{2,1,0:T(2,128)(2,1)S(1)}, bf16[2,2,128]{2,1,0:T(2,128)(2,1)}, u32[]{:S(2)}) copy-start(bf16[2,2,128]{2,1,0:T(2,128)(2,1)} %param.11) | copy-start | bytes 3076
  143.6 27.3 %copy-start.35 = (bf16[2,2,128]{2,1,0:T(2,128)(2,1)S(1)}, bf16[2,2,128]{2,1,0:T(2,128)(2,1)}, u32[]{:S(2)}) copy-start(bf16[2,2,128]{2,1,0:T(2,128)(2,1)} %param.13) | copy-start | bytes 3076
  165.1 40.2 %all-to-all-start.5 = ((bf16[2,8,2,176,256]{4,1,0,2,3:T(8,128)(2,1)}), bf16[2,8,2,176,256]{4,1,0,2,3:T(8,128)(2,1)S(1)}, u32[]{:S(2)}, u32[]{:S(2)}) async-start(bf16[2,8,2,176,256]{4,1,0,2,3:T(8,128)(2,1)} %copy.320), calls=%async_computation.5 | async-start | bytes 5767168 | tf_op jit(solution)/shard_map/all_to_all | solution.py:184
  182.3 4.5 copy-start.27
  186.8 2.5 copy-start.10
  186.8 2.5 copy-start.13
  215.0 9.7 %copy-start.6 = (bf16[2,128,11,2,128]{4,1,2,0,3:T(8,128)(2,1)}, bf16[2,128,11,2,128]{4,1,2,0,3:T(8,128)(2,1)S(1)}, u32[]{:S(2)}) copy-start(bf16[2,128,11,2,128]{4,1,2,0,3:T(8,128)(2,1)S(1)} %get-tuple-element.26) | copy-start | bytes 4325380
  215.0 2.8 copy-start.24
  215.0 2.8 copy-start.36
  219.6 2.9 copy-start.8
  224.0 8.1 %copy-start.16 = (bf16[2,128,11,2,128]{1,4,2,0,3:T(8,128)(2,1)}, bf16[2,128,11,2,128]{1,4,2,0,3:T(8,128)(2,1)S(1)}, u32[]{:S(2)}) copy-start(bf16[2,128,11,2,128]{1,4,2,0,3:T(8,128)(2,1)S(1)} %get-tuple-element.11) | copy-start | bytes 4325380
  227.8 3.8 copy-start.19
  231.6 3.6 copy-start.17
  251.1 40.0 %all-to-all-start.6 = ((bf16[2,128,2,11,256]{4,2,3,0,1:T(2,128)(2,1)}), bf16[2,128,2,11,256]{4,2,3,0,1:T(2,128)(2,1)S(1)}, u32[]{:S(2)}, u32[]{:S(2)}) async-start(bf16[2,128,2,11,256]{4,2,3,0,1:T(2,128)(2,1)} %copy.339), calls=%async_computation.6 | async-start | bytes 5767168 | tf_op jit(solution)/shard_map/all_to_all | solution.py:190
  292.7 40.2 %all-to-all-start.2 = ((bf16[2,128,2,11,256]{4,2,3,0,1:T(2,128)(2,1)}), bf16[2,128,2,11,256]{4,2,3,0,1:T(2,128)(2,1)S(1)}, u32[]{:S(2)}, u32[]{:S(2)}) async-start(bf16[2,128,2,11,256]{4,2,3,0,1:T(2,128)(2,1)} %copy.309), calls=%async_computation.2 | async-start | bytes 5767168 | tf_op jit(solution)/shard_map/all_to_all | solution.py:174
  297.3 3.3 copy-start.5
  332.8 7.9 %copy-start.40 = (f32[2,128,128]{2,1,0:T(8,128)S(1)}, f32[2,128,128]{2,1,0:T(8,128)}, u32[]{:S(2)}) copy-start(f32[2,128,128]{2,1,0:T(8,128)} %fusion.100) | copy-start | bytes 393220
  334.4 38.3 %all-to-all-start.7 = ((bf16[2,8,360,256]{3,1,0,2:T(8,128)(2,1)}), bf16[2,8,360,256]{3,1,0,2:T(8,128)(2,1)S(1)}, u32[]{:S(2)}, u32[]{:S(2)}) async-start(bf16[2,8,360,256]{3,1,0,2:T(8,128)(2,1)} %copy.343), calls=%async_computation.7 | async-start | bytes 5898240 | tf_op jit(solution)/shard_map/all_to_all | solution.py:193
  338.1 2.7 copy-start.9
  338.1 4.7 copy-start.7
  338.1 4.7 copy-start.20
  342.8 2.4 copy-start.22
  352.6 25.5 %copy-start.38 = (bf16[2,128]{1,0:T(2,128)(2,1)S(1)}, bf16[2,128]{1,0:T(2,128)(2,1)}, u32[]{:S(2)}) copy-start(bf16[2,128]{1,0:T(2,128)(2,1)} %get-tuple-element.34) | copy-start | bytes 1540
  352.6 25.5 %copy-start.39 = (bf16[2,128]{1,0:T(2,128)(2,1)S(1)}, bf16[2,128]{1,0:T(2,128)(2,1)}, u32[]{:S(2)}) copy-start(bf16[2,128]{1,0:T(2,128)(2,1)} %get-tuple-element.32) | copy-start | bytes 1540
  352.6 25.6 %copy-start.33 = (bf16[2,128]{1,0:T(2,128)(2,1)S(1)}, bf16[2,128]{1,0:T(2,128)(2,1)}, u32[]{:S(2)}) copy-start(bf16[2,128]{1,0:T(2,128)(2,1)} %get-tuple-element.10) | copy-start | bytes 1540
  372.7 121.0 %all-to-all-start.3 = ((bf16[2,8,360,256]{3,1,0,2:T(8,128)(2,1)}), bf16[2,8,360,256]{3,1,0,2:T(8,128)(2,1)}, u32[]{:S(2)}, u32[]{:S(2)}) async-start(bf16[2,8,360,256]{3,1,0,2:T(8,128)(2,1)} %copy.313), calls=%async_computation.3 | async-start | bytes 5898240 | tf_op jit(solution)/shard_map/all_to_all | solution.py:177
  377.4 107.8 %all-reduce.4.cloned.1.call-start = ((), (), s32[]{:S(2)}) async-start(), calls=%async_computation.8 | async-start | bytes 524288 | tf_op jit(solution)/shard_map/psum | solution.py:202
  (18 other events, 29.5 us)
Sparse Core Ops, SparseCore 0:
  382.1 103.0 all-reduce.3
where the time goes:
time: 515 us; the launch traced here: 508 us
  waiting for transfers between devices  214 us (42%)
  local copies, waits for them, and re-layouts  95.7 us (19%)
  blocking collectives  65.8 us (13%)
  matrix products  54.2 us (11%)
  starting transfers between devices  41.3 us (8%)
  other arithmetic  21.8 us (4%)
  between operations  15 us (3%)
    psum x1, blocking collectives, per_device(): lax.psum(first_bias_local.astype(jnp.bfloat16), ('lat', 'batch'))  65.8 us
    dot_general x32, matrix products, contract(): return jnp.einsum(pattern, left, right, preferred_element_type=jnp.float32)  54.2 us
    all_to_all x1, waiting for transfers between devices, per_device(): lax.all_to_all(inputs, 'lon', split_axis=3, concat_axis=2, tiled=True)  40.3 us
    psum x1, waiting for transfers between devices, per_device(): lax.psum(first_local.astype(jnp.bfloat16), ('lat', 'batch'))  40 us
    all_to_all x1, waiting for transfers between devices, per_device(): lax.all_to_all(weighted, 'lon', split_axis=3, concat_axis=2, tiled=True)  33.3 us
    all_to_all x1, waiting for transfers between devices, per_device(): lax.all_to_all(spatial, 'lat', split_axis=1, concat_axis=3, tiled=True)  26.8 us
    all_to_all x1, waiting for transfers between devices, per_device(): lax.all_to_all(half_modes, 'lat', split_axis=3, concat_axis=1, tiled=True)  21.5 us
    all_to_all x1, waiting for transfers between devices, per_device(): lax.all_to_all(pencil_grad, 'lon', split_axis=2, concat_axis=3, tiled=True)  20.1 us
  transfers between devices with their start and end apart: 9, of which 8 were waited for; matrix products, arithmetic and copies ran while one was open for 21% of the time, Pallas kernels for 0%

commit v1 on v0

v1 whole, which is shorter than its diff:
```python
import functools
import math

import jax
import jax.numpy as jnp
import numpy as np
from jax import lax
from jax.experimental import pallas as pl
from jax.experimental.pallas import tpu as pltpu
from jax.sharding import PartitionSpec as P

MESH = pl.DeviceIdType.MESH
MODES = 176
LON = 360
LAT = 128
NLAT = 16
NLON = 4
ROWS = 8
MAIN = 80
REST = 10
KL = 11
WINDOW = 32
CHUNKS = 8
HALF = 4
SPAN = 2 * MODES
LINES = KL * LAT
BF = jnp.bfloat16
F32 = jnp.float32


def window_start(h):
    return min(REST * h // 16 * 16, MAIN - WINDOW)


def build_tables():
    w = np.arange(LON)[:, None]
    k = np.arange(MODES)[None, :]
    angle = (w * k % LON).astype(np.float32) * np.float32(2.0 * math.pi / LON)
    cos = np.cos(angle) / math.sqrt(LON)
    sin = np.sin(angle) / math.sqrt(LON)
    weight = np.where(k == 0, 1.0, 2.0)
    forward = np.concatenate([cos, -sin], axis=1)
    back = np.concatenate([weight * cos, -weight * sin], axis=1)

    def arranged(table):
        here = table.reshape(NLON, MAIN + REST, SPAN)
        main = here[:, :MAIN].reshape(NLON * MAIN, SPAN)
        rest = np.zeros((ROWS, NLON, WINDOW, SPAN))
        for h in range(ROWS):
            at = REST * h - window_start(h)
            rest[h, :, at : at + REST] = here[:, MAIN:]
        return main, rest.reshape(ROWS, NLON * WINDOW, SPAN)

    first, second, main_out, rest_out = [], [], [], []
    for there, home in ((forward, back), (back, forward)):
        main, rest = arranged(there)
        first.append(main[:256].T)
        second.append(
            np.stack([np.concatenate([main[256:], rest[h]], axis=0).T for h in range(ROWS)])
        )
        main, rest = arranged(home)
        main_out.append(main)
        rest_out.append(rest)
    h = np.arange(LAT)
    angle = (h[:, None] * h[None, :] % LAT).astype(np.float32) * np.float32(2.0 * math.pi / LAT)
    c = np.cos(angle) / math.sqrt(LAT)
    s = np.sin(angle) / math.sqrt(LAT)
    square = np.stack([np.stack([c, -s], axis=1), np.stack([s, c], axis=1)], axis=0)
    square = square.reshape(2, NLAT, ROWS, 2, LAT).transpose(1, 0, 2, 3, 4).reshape(256, 256)
    cast = lambda a: np.asarray(a, np.float32).astype(jnp.bfloat16)
    return (
        cast(np.stack(first)),
        cast(np.stack(second)),
        cast(np.stack(main_out)),
        cast(np.stack(rest_out)),
        cast(square.T),
        cast(square),
    )


def dot(a, b):
    return jnp.dot(a, b, preferred_element_type=F32)


def dot_tn(a, b):
    return lax.dot_general(a, b, (((0,), (0,)), ((), ())), preferred_element_type=F32)


def kernel(
    x_ref, g_ref, xr_ref, gr_ref, area_ref, w1_ref, b1_ref, w2_ref, b2_ref,
    first_hbm, second_hbm, main_hbm, rest_hbm, latf_ref, latb_ref,
    out_main, out_rest, gw_ref, gb_ref,
    first, second, main_tab, rest_tab,
    ybuf, l1s, l1r, l2s, l2r, y2s, tmp, tmp2, racc,
    sa, hs, gps, sls, shb, dbuf1, dbuf2, wc, wt, bias, acc1, acc2, accb,
    gsend, grecv, xs, xr, ag, brows,
    y1_s, y1_r, l1_s, l1_r, l2_s, l2_r, y2_s, y2_r, t_s, g_s, g_r, p_s, p_r, a_s, a_r,
):
    me = lax.axis_index("lat")
    col = lax.axis_index("lon")
    member = lax.axis_index("batch")

    tables = [
        pltpu.make_async_copy(src, dst, t_s.at[i])
        for i, (src, dst) in enumerate(
            ((first_hbm, first), (second_hbm, second), (main_hbm, main_tab), (rest_hbm, rest_tab))
        )
    ]
    for copy in tables:
        copy.start()

    barrier = pltpu.get_barrier_semaphore()

    def greet_lat(i, _):
        pl.semaphore_signal(
            barrier, inc=1, device_id={"lat": lax.rem(me + i, NLAT)}, device_id_type=MESH
        )
        return 0

    lax.fori_loop(1, NLAT, greet_lat, 0)
    for i in range(1, NLON):
        pl.semaphore_signal(
            barrier, inc=1, device_id={"lon": lax.rem(col + i, NLON)}, device_id_type=MESH
        )
    pl.semaphore_signal(barrier, inc=1, device_id={"batch": 1 - member}, device_id_type=MESH)
    pl.semaphore_wait(barrier, NLAT - 1 + NLON - 1 + 1)

    def place(t):
        c = lax.rem(t, HALF)
        return c // 2, lax.rem(c, 2)

    def y1_from(t, field, rest):
        b, n = place(t)
        for i in (2, 1, 3, 0):
            j = lax.rem(col + i, NLON)
            lanes = pl.ds(pl.multiple_of((2 * j + n) * 128, 128), 128)
            pairs = (
                (field.at[b, :, pl.ds(0, MAIN), lanes], ybuf.at[t, col, pl.ds(0, ROWS)]),
                (rest.at[b, :, lanes], ybuf.at[t, col, ROWS]),
            )
            for src, dst in pairs:
                if i:
                    pltpu.make_async_remote_copy(
                        src, dst, y1_s.at[t], y1_r.at[t],
                        device_id={"lon": j}, device_id_type=MESH,
                    ).start()
                else:
                    pltpu.make_async_copy(src, dst, y1_r.at[t]).start()

    def y1_send(t):
        @pl.when(t < HALF)
        def _():
            y1_from(t, x_ref, xr_ref)

        @pl.when(t >= HALF)
        def _():
            y1_from(t, g_ref, gr_ref)

    def wait_bytes(ref, sem):
        pltpu.make_async_copy(ref, ref, sem).wait()

    y1_send(0)
    y1_send(1)

    for i, ref in enumerate((w1_ref, w2_ref)):
        for n in range(2):
            re = ref[0, n].astype(F32)
            im = ref[1, n].astype(F32)
            whole = jnp.concatenate(
                [jnp.concatenate([re, im], axis=1), jnp.concatenate([-im, re], axis=1)], axis=0
            )
            wc[i, n] = whole.astype(BF)
            wt[i, n] = whole.T.astype(BF)
    for i, ref in enumerate((b1_ref, b2_ref)):
        for n in range(2):
            for q in range(2):
                bias[i, n, :, q * 128 : (q + 1) * 128] = ref[q, n : n + 1].astype(F32)
    acc1[...] = jnp.zeros_like(acc1)
    acc2[...] = jnp.zeros_like(acc2)
    accb[...] = jnp.zeros_like(accb)
    for copy in tables:
        copy.wait()

    def rest_window(h):
        return pl.multiple_of(jnp.minimum(REST * h // 16 * 16, MAIN - WINDOW), 16)

    def stage_a(t):
        kind = t // HALF
        slot = lax.rem(t, 2)
        wait_bytes(ybuf.at[t], y1_r.at[t])

        @pl.when(t + 2 < CHUNKS)
        def _():
            y1_send(t + 2)

        def row(h, _):
            cols = ybuf[t, :, h].reshape(NLON * MAIN, 128)
            rest = ybuf[t, :, ROWS, pl.ds(rest_window(h), WINDOW), :].reshape(NLON * WINDOW, 128)
            tail = jnp.concatenate([cols[256:], rest], axis=0)
            modes = dot(first[kind], cols[:256]) + dot(second[kind, h], tail)
            scale = jnp.where(kind == 0, 1.0, area_ref[h])
            tmp[pl.ds(pl.multiple_of(h * SPAN, 8), SPAN), :] = modes * scale
            return 0

        lax.fori_loop(0, ROWS, row, 0)

        @pl.when(t >= 2)
        def _():
            wait_bytes(l1s.at[slot, pl.ds(0, NLAT - 1)], l1_s.at[t - 2])

        def peer(i, _):
            l = lax.rem(me + i, NLAT)
            for kk in range(KL):
                k = l * KL + kk
                tile = jnp.concatenate(
                    [
                        tmp[pl.ds(k, ROWS, stride=SPAN), :],
                        tmp[pl.ds(k + MODES, ROWS, stride=SPAN), :],
                    ],
                    axis=0,
                ).astype(BF)
                l1s[slot, l, kk] = tile

            @pl.when(i > 0)
            def _():
                pltpu.make_async_remote_copy(
                    l1s.at[slot, l], l1r.at[t, me], l1_s.at[t], l1_r.at[t],
                    device_id={"lat": l}, device_id_type=MESH,
                ).start()

            return 0

        lax.fori_loop(0, NLAT, peer, 0)
        l1r[t, me] = l1s[slot, me]

    def lat_forward(t, out, at):
        def one(k, _):
            z = l1r[t, :, k].reshape(256, 128)
            sp = dot(latf_ref[...], z).astype(BF)
            rows = pl.ds(pl.multiple_of(k * LAT, LAT), LAT)
            view = out.at[at] if at is not None else out
            view[rows, 0:128] = sp[:128]
            view[rows, 128:256] = sp[128:]
            return 0

        lax.fori_loop(0, KL, one, 0)

    def lat_back(t, slot):
        @pl.when(t >= 2)
        def _():
            wait_bytes(l2s.at[slot, pl.ds(0, NLAT - 1)], l2_s.at[t - 2])

        def one(k, _):
            rows = pl.ds(pl.multiple_of(k * LAT, LAT), LAT)
            s = jnp.concatenate([shb[rows, 0:128], shb[rows, 128:256]], axis=0)
            l2s[slot, :, k] = dot(latb_ref[...], s).astype(BF).reshape(NLAT, 16, 128)
            return 0

        lax.fori_loop(0, KL, one, 0)

        def peer(i, _):
            l = lax.rem(me + i, NLAT)
            pltpu.make_async_remote_copy(
                l2s.at[slot, l], l2r.at[t, me], l2_s.at[t], l2_r.at[t],
                device_id={"lat": l}, device_id_type=MESH,
            ).start()
            return 0

        lax.fori_loop(1, NLAT, peer, 0)
        l2r[t, me] = l2s[slot, me]

    BLOCK = 176
    C0 = math.sqrt(2.0 / math.pi)
    C1 = C0 * 0.044715

    def stage_b_forward(t):
        n = lax.rem(t, 2)
        slot = lax.rem(t, 2)
        lat_forward(t, sa, t)

        def one(i, _):
            rows = pl.ds(pl.multiple_of(i * BLOCK, 16), BLOCK)
            u = dot(sa[t, rows], wc[0, n]) + bias[0, n]
            sq = u * u
            th = jnp.tanh(u * (C0 + C1 * sq))
            half = 0.5 + 0.5 * th
            hid = (u * half).astype(BF)
            hs[t, rows] = hid
            gps[t, rows] = half + (0.5 * u) * (1.0 - th * th) * (C0 + (3.0 * C1) * sq)
            o = dot(hid, wc[1, n]) + bias[1, n]
            slope = jnp.tanh(o * 4.0)
            sls[t, rows] = slope * slope
            shb[rows] = (o - 0.25 * slope).astype(BF)
            return 0

        lax.fori_loop(0, LINES // BLOCK, one, 0)
        lat_back(t, slot)

    def stage_b_backward(t):
        c = t - HALF
        n = lax.rem(t, 2)
        slot = lax.rem(t, 2)
        lat_forward(t, dbuf2, None)

        def one(i, _):
            rows = pl.ds(pl.multiple_of(i * BLOCK, 16), BLOCK)
            d = (dbuf2[rows].astype(F32) * sls[c, rows]).astype(BF)
            dbuf2[rows] = d
            dp = (dot(d, wt[1, n]) * gps[c, rows]).astype(BF)
            dbuf1[rows] = dp
            shb[rows] = dot(dp, wt[0, n]).astype(BF)
            accb[n, 0] += jnp.sum(dp.astype(F32), axis=0, keepdims=True)
            accb[n, 1] += jnp.sum(d.astype(F32), axis=0, keepdims=True)
            return 0

        lax.fori_loop(0, LINES // BLOCK, one, 0)
        lat_back(t, slot)
        acc1[n] += dot_tn(sa[c], dbuf1[...])
        acc2[n] += dot_tn(hs[c], dbuf2[...])

    def stage_c(t):
        kind = t // HALF
        slot = lax.rem(t, 2)
        b, n = place(t)
        wait_bytes(l2r.at[t, pl.ds(0, NLAT - 1)], l2_r.at[t])

        def peer(l, _):
            for kk in range(KL):
                k = l * KL + kk
                v = l2r[t, l, kk].astype(F32)
                tmp2[pl.ds(k, ROWS, stride=SPAN), :] = v[:ROWS]
                tmp2[pl.ds(k + MODES, ROWS, stride=SPAN), :] = v[ROWS:]
            return 0

        lax.fori_loop(0, NLAT, peer, 0)

        @pl.when(t >= 2)
        def _():
            wait_bytes(y2s.at[slot], y2_s.at[t - 2])

        racc[...] = jnp.zeros_like(racc)

        def row(h, _):
            s = tmp2[pl.ds(pl.multiple_of(h * SPAN, 8), SPAN), :].astype(BF)
            y2s[slot, :, h] = dot(main_tab[kind], s).astype(BF).reshape(NLON, MAIN, 128)
            racc[:, pl.ds(rest_window(h), WINDOW), :] += dot(rest_tab[kind, h], s).reshape(
                NLON, WINDOW, 128
            )
            return 0

        lax.fori_loop(0, ROWS, row, 0)
        y2s[slot, :, ROWS] = racc[...].astype(BF)
        lanes = pl.ds(pl.multiple_of((2 * col + n) * 128, 128), 128)
        for i in (2, 1, 3, 0):
            j = lax.rem(col + i, NLON)
            pairs = (
                (y2s.at[slot, j, pl.ds(0, ROWS)], out_main.at[kind, b, :, :, lanes]),
                (y2s.at[slot, j, ROWS], out_rest.at[kind, b, :, lanes]),
            )
            for src, dst in pairs:
                if i:
                    pltpu.make_async_remote_copy(
                        src, dst, y2_s.at[t], y2_r.at[t],
                        device_id={"lon": j}, device_id_type=MESH,
                    ).start()
                else:
                    pltpu.make_async_copy(src, dst, y2_s.at[t]).start()

    def scatter_grads():
        gsend[...] = jnp.zeros_like(gsend)
        brows[...] = jnp.zeros_like(brows)
        for which, acc in enumerate((acc1, acc2)):
            for n in range(2):
                a = acc[n]
                parts = (
                    a[:128, :128] + a[128:, 128:],
                    a[:128, 128:] - a[128:, :128],
                )
                for q in range(2):
                    at = (which * 2 + q) * 2 + n
                    part = parts[q].astype(BF)
                    gsend[2 * at, 0:64] = part[:64]
                    gsend[2 * at + 1, 0:64] = part[64:]
                    brows[at : at + 1, :] = accb[n, which, :, q * 128 : (q + 1) * 128]
        gsend[0, 64:80] = brows[...].astype(BF)

        def peer(i, _):
            l = lax.rem(me + i, NLAT)
            pltpu.make_async_remote_copy(
                gsend.at[l], grecv.at[me], g_s, g_r,
                device_id={"lat": l}, device_id_type=MESH,
            ).start()
            return 0

        lax.fori_loop(1, NLAT, peer, 0)
        grecv[me] = gsend[me]

    def finish_grads():
        wait_bytes(grecv.at[pl.ds(0, NLAT - 1)], g_r)
        part = grecv[0].astype(F32)
        for l in range(1, NLAT):
            part = part + grecv[l].astype(F32)
        xs[...] = part
        swap = pltpu.make_async_remote_copy(
            xs, xr, p_s, p_r, device_id={"batch": 1 - member}, device_id_type=MESH
        )
        swap.start()
        swap.wait()
        factor = 1.0 / math.sqrt(4 * LAT * MODES)
        ag[me] = ((xs[...] + xr[...]) * factor).astype(BF)

        def peer(i, _):
            l = lax.rem(me + i, NLAT)
            pltpu.make_async_remote_copy(
                ag.at[me], ag.at[me], a_s, a_r,
                device_id={"lat": l}, device_id_type=MESH,
            ).start()
            return 0

        lax.fori_loop(1, NLAT, peer, 0)
        wait_bytes(ag.at[pl.ds(0, NLAT - 1)], a_r)
        for l in range(NLAT):
            gw_ref[l * 64 : (l + 1) * 64, :] = ag[l, 0:64].astype(F32)
        gb_ref[...] = ag[0, 64:80].astype(F32)[:8]
        wait_bytes(ag.at[pl.ds(0, NLAT - 1)], a_s)
        wait_bytes(gsend.at[pl.ds(0, NLAT - 1)], g_s)

    def slot_of(s, _):
        @pl.when(s < CHUNKS)
        def _():
            stage_a(s)

        @pl.when(jnp.logical_and(s >= 1, s <= CHUNKS))
        def _():
            t = s - 1
            wait_bytes(l1r.at[t, pl.ds(0, NLAT - 1)], l1_r.at[t])

            @pl.when(t < HALF)
            def _():
                stage_b_forward(t)

            @pl.when(t >= HALF)
            def _():
                stage_b_backward(t)

        @pl.when(s == CHUNKS)
        def _():
            scatter_grads()

        @pl.when(s >= 2)
        def _():
            stage_c(s - 2)

        return 0

    lax.fori_loop(0, CHUNKS + 2, slot_of, 0)
    finish_grads()
    for t in range(CHUNKS):
        wait_bytes(ybuf.at[t, pl.ds(0, NLON - 1)], y1_s.at[t])
        wait_bytes(ybuf.at[t, pl.ds(0, NLON - 1)], y2_r.at[t])
    for t in (CHUNKS - 2, CHUNKS - 1):
        wait_bytes(l1s.at[t % 2, pl.ds(0, NLAT - 1)], l1_s.at[t])
        wait_bytes(l2s.at[t % 2, pl.ds(0, NLAT - 1)], l2_s.at[t])
        wait_bytes(y2s.at[t % 2], y2_s.at[t])


def per_device(inputs, cotangent, area, w1, b1, w2, b2):
    members, rows, cols, channels = inputs.shape
    tables = [jnp.asarray(a) for a in build_tables()]
    x_rest = inputs[:, :, MAIN:, :].reshape(members, rows * REST, channels)
    g_rest = cotangent[:, :, MAIN:, :].reshape(members, rows * REST, channels)
    anywhere = pl.BlockSpec(memory_space=pl.ANY)
    vmem = pl.BlockSpec(memory_space=pltpu.VMEM)
    smem = pl.BlockSpec(memory_space=pltpu.SMEM)
    dma = pltpu.SemaphoreType.DMA
    V = pltpu.VMEM
    out_main, out_rest, gw, gb = pl.pallas_call(
        kernel,
        out_shape=(
            jax.ShapeDtypeStruct((2, members, rows, MAIN, channels), BF),
            jax.ShapeDtypeStruct((2, members, rows * REST, channels), BF),
            jax.ShapeDtypeStruct((1024, 128), F32),
            jax.ShapeDtypeStruct((8, 128), F32),
        ),
        in_specs=[anywhere] * 4 + [smem] + [vmem] * 4 + [anywhere] * 4 + [vmem] * 2,
        out_specs=(anywhere, anywhere, vmem, vmem),
        scratch_shapes=[
            V((2, SPAN, 256), BF),
            V((2, ROWS, SPAN, 192), BF),
            V((2, NLON * MAIN, SPAN), BF),
            V((2, ROWS, NLON * WINDOW, SPAN), BF),
            V((CHUNKS, NLON, ROWS + 1, MAIN, 128), BF),
            V((2, NLAT, KL, 16, 128), BF),
            V((CHUNKS, NLAT, KL, 16, 128), BF),
            V((2, NLAT, KL, 16, 128), BF),
            V((CHUNKS, NLAT, KL, 16, 128), BF),
            V((2, NLON, ROWS + 1, MAIN, 128), BF),
            V((ROWS * SPAN, 128), F32),
            V((ROWS * SPAN, 128), F32),
            V((NLON, MAIN, 128), F32),
            V((HALF, LINES, 256), BF),
            V((HALF, LINES, 256), BF),
            V((HALF, LINES, 256), F32),
            V((HALF, LINES, 256), F32),
            V((LINES, 256), BF),
            V((LINES, 256), BF),
            V((LINES, 256), BF),
            V((2, 2, 256, 256), BF),
            V((2, 2, 256, 256), BF),
            V((2, 2, 1, 256), F32),
            V((2, 256, 256), F32),
            V((2, 256, 256), F32),
            V((2, 2, 1, 256), F32),
            V((NLAT, 80, 128), BF),
            V((NLAT, 80, 128), BF),
            V((80, 128), F32),
            V((80, 128), F32),
            V((NLAT, 80, 128), BF),
            V((16, 128), F32),
        ]
        + [dma((CHUNKS,))] * 8
        + [dma((4,))]
        + [dma(())] * 6,
        compiler_params=pltpu.CompilerParams(
            collective_id=0, has_side_effects=True, vmem_limit_bytes=60 * 2**20
        ),
        name="afno",
    )(inputs, cotangent, x_rest, g_rest, area, w1, b1, w2, b2, *tables)

    def whole(kind):
        rest = out_rest[kind].reshape(members, rows, REST, channels)
        return jnp.concatenate([out_main[kind], rest], axis=2).astype(F32)

    weighted = (area[None, :, None, None] * cotangent.astype(F32)).astype(BF)
    output_field = (inputs.astype(F32) + whole(0)).astype(BF)
    grad_input = (weighted.astype(F32) + whole(1)).astype(BF)
    gw = gw.reshape(2, 2, 2, 128, 128)
    gb = gb.reshape(2, 2, 2, 128)
    return output_field, grad_input, gw[0], gw[1], gb[0], gb[1]


def solution(mesh):
    return jax.shard_map(
        per_device,
        mesh=mesh,
        in_specs=(
            P("batch", "lat", "lon", None),
            P("batch", "lat", "lon", None),
            P("lat"),
            P(None, "lon", None, None),
            P(None, "lon", None),
            P(None, "lon", None, None),
            P(None, "lon", None),
        ),
        out_specs=(
            P("batch", "lat", "lon", None),
            P("batch", "lat", "lon", None),
            P(None, "lon", None, None),
            P(None, "lon", None, None),
            P(None, "lon", None),
            P(None, "lon", None),
        ),
        check_vma=False,
    )
```

time: 515 us -> 203 us (0.39); the launches traced: 508 us -> 203 us
  waiting for transfers between devices: 214 us -> 0 us
  Pallas kernels: 0 us -> 170 us
  local copies, waits for them, and re-layouts: 95.7 us -> 23.1 us
  blocking collectives: 65.8 us -> 0 us
  matrix products: 54.2 us -> 0 us
  starting transfers between devices: 41.3 us -> 0 us
  between operations: 15 us -> 0.79 us
  other arithmetic: 21.8 us -> 8.9 us
    all_to_all x8 -> x0, waiting for transfers between devices: 174 us -> none  [the longest x1 40.3 us: per_device(): lax.all_to_all(inputs, 'lon', split_axis=3, concat_axis=2, tiled=True)]
    pallas_call x0 -> x1, Pallas kernels: none -> 170 us  [per_device(): pl.pallas_call(kernel, out_shape=(jax.ShapeDtypeStruct((2, members, rows,...]
    psum x1 -> x0, blocking collectives: 65.8 us -> none  [per_device(): lax.psum(first_bias_local.astype(jnp.bfloat16), ('lat', 'batch'))]
    dot_general x32 -> x0, matrix products: 54.2 us -> none  [contract(): return jnp.einsum(pattern, left, right, preferred_element_type=jnp.float32)]
    all_to_all x8 -> x0, starting transfers between devices: 41.2 us -> none  [the longest x1 9.15 us: per_device(): lax.all_to_all(half_modes, 'lat', split_axis=3, concat_axis=1, tiled=True)]
    psum x1 -> x0, waiting for transfers between devices: 40 us -> none  [per_device(): lax.psum(first_local.astype(jnp.bfloat16), ('lat', 'batch'))]
    convert_element_type x10 -> x0, local copies, waits for them, and re-layouts: 29.4 us -> none  [the longest x2 9.09 us: back_lat(): contract('bmqkc,phqm->bhpkc', modes_block, lat_square).astype(jnp.bfloat16)]
    all_to_all x10 -> x0, local copies, waits for them, and re-layouts: 20.6 us -> none  [the longest x2 8.49 us: per_device(): lax.all_to_all(inputs, 'lon', split_axis=3, concat_axis=2, tiled=True)]
  transfers between devices with their start and end apart: 9 -> 0, of which waited for: 8 -> 0; matrix products, arithmetic and copies ran while one was open for 21% -> 0% of each run, Pallas kernels for 0% -> 0%
where the time goes in v1:
time: 203 us
  Pallas kernels  170 us (84%)
  local copies, waits for them, and re-layouts  23.1 us (11%)
  other arithmetic  8.9 us (4%)
    pallas_call x1, Pallas kernels, per_device(): pl.pallas_call(kernel, out_shape=(jax.ShapeDtypeStruct((2, members, rows,...  170 us
    unnamed x18, local copies, waits for them, and re-layouts  13.1 us
    convert_element_type x1, other arithmetic, per_device(): grad_input = (weighted.astype(F32) + whole(1)).astype(BF)  8.9 us

profile of v1, /device:TPU:1, one launch (start us, length us, event | category | flops | bytes accessed | tf_op | source)
XLA Modules:
  0.0 202.7 jit_solution(5155197159151067604)
XLA Ops:
  0.6 0.0 copy-start
  0.6 1.1 slice.34
  1.8 0.3 copy.28
  2.1 0.8 copy.32.xr_ref
  2.9 1.0 slice.35
  3.9 0.3 copy.29
  4.3 0.8 copy.33.gr_ref
  5.1 0.0 copy-done
  5.1 3.3 %copy.27.x_ref = bf16[2,8,90,1024]{3,2,1,0:T(8,128)(2,1)} copy(bf16[2,8,90,1024]{3,1,2,0:T(8,128)(2,1)S(1)} %copy-done) | data formatting | bytes 5898240 | tf_op args[0]
  8.4 0.0 copy-done.1
  8.4 3.4 %copy.31.g_ref = bf16[2,8,90,1024]{3,2,1,0:T(8,128)(2,1)} copy(bf16[2,8,90,1024]{3,1,2,0:T(8,128)(2,1)S(1)} %copy-done.1) | data formatting | bytes 5898240 | tf_op args[1]
  11.7 169.9 %afno.1 = (bf16[2,2,8,80,1024]{4,3,2,1,0:T(8,128)(2,1)}, bf16[2,2,80,1024]{3,2,1,0:T(8,128)(2,1)}, f32[1024,128]{1,0:T(8,128)}, f32[8,128]{1,0:T(8,128)}) custom-call(bf16[2,8,90,1024]{3,2,1,0:T(8,128)(2,1)} %copy.27.x_ref, bf16[2,8,90,1024]{3,2,1,0:T(8,128)(2,1)} %copy.31.g_ref, bf16[2,80,1024]{2,1,0:T(8,128)(2,1)} %copy.32.xr_ref, ...), custom_call_target="tpu_custom_call" | custom-call | tf_op jit(solution)/shard_map/afno/pallas_call | solution.py:477
  181.6 0.0 copy-start.5
  181.7 0.0 copy-start.4
  181.7 0.0 copy-start.3
  181.7 3.3 %slice_bitcast_fusion = (bf16[2,8,80,1024]{3,2,1,0:T(8,128)(2,1)S(1)}, bf16[2,8,80,1024]{3,2,1,0:T(8,128)(2,1)S(1)}) fusion(bf16[2,2,8,80,1024]{4,3,2,1,0:T(8,128)(2,1)} %get-tuple-element.10), kind=kLoop, calls=%fused_computation.3 | loop fusion | bytes 10485760 | tf_op jit(solution)/shard_map/squeeze | solution.py:532
  185.0 0.0 copy-start.2
  185.0 0.0 copy-start.6
  185.0 0.0 copy-done.5
  185.0 0.6 fusion.2
  185.6 0.0 copy-done.4
  185.6 0.8 fusion.1
  186.4 0.0 copy-done.3
  186.5 0.3 copy.37
  186.8 0.1 copy.38
  186.9 0.3 copy.34
  187.3 0.1 copy.35
  187.4 0.0 copy-done.2
  187.4 0.0 copy-done.6
  187.4 8.9 %add_convert_fusion = (bf16[2,8,90,1024]{3,2,1,0:T(8,128)(2,1)S(1)}, bf16[2,8,90,1024]{3,2,1,0:T(8,128)(2,1)S(1)}) fusion(bf16[2,8,10,1024]{3,2,1,0:T(8,128)(2,1)S(1)} %copy.38, bf16[2,8,80,1024]{3,2,1,0:T(8,128)(2,1)S(1)} %get-tuple-element.26, f32[8]{0:T(128)S(1)} %copy-done.6, bf16[2,8,90,1024]{3,1,2,0:T(8,128)(2,1)S(1)} %copy-done.2, ...), kind=kLoop, calls=%fused_computation | loop fusion | flops 25067520 | bytes 17694752 | tf_op jit(solution)/shard_map/convert_element_type | solution.py:536
  196.3 3.2 %copy.40 = bf16[2,8,90,1024]{3,1,2,0:T(8,128)(2,1)} copy(bf16[2,8,90,1024]{3,2,1,0:T(8,128)(2,1)S(1)} %get-tuple-element.34) | data formatting | bytes 5898240
  199.5 3.2 %copy.39 = bf16[2,8,90,1024]{3,1,2,0:T(8,128)(2,1)} copy(bf16[2,8,90,1024]{3,2,1,0:T(8,128)(2,1)S(1)} %get-tuple-element.35) | data formatting | bytes 5898240
  (2 shorter events, 0.0 us)
Async XLA Ops:
  0.6 4.4 %copy-start = (bf16[2,8,90,1024]{3,1,2,0:T(8,128)(2,1)S(1)}, bf16[2,8,90,1024]{3,1,2,0:T(8,128)(2,1)}, u32[]{:S(2)}) copy-start(bf16[2,8,90,1024]{3,1,2,0:T(8,128)(2,1)} %param.13) | copy-start | bytes 8847364
  5.1 3.3 %copy-start.1 = (bf16[2,8,90,1024]{3,1,2,0:T(8,128)(2,1)S(1)}, bf16[2,8,90,1024]{3,1,2,0:T(8,128)(2,1)}, u32[]{:S(2)}) copy-start(bf16[2,8,90,1024]{3,1,2,0:T(8,128)(2,1)} %param.14) | copy-start | bytes 8847364
  181.6 3.3 %copy-start.5 = (f32[8,128]{1,0:T(8,128)S(1)}, f32[8,128]{1,0:T(8,128)}, u32[]{:S(2)}) copy-start(f32[8,128]{1,0:T(8,128)} %get-tuple-element.13) | copy-start | bytes 12292
  181.7 3.9 %copy-start.4 = (f32[1024,128]{1,0:T(8,128)S(1)}, f32[1024,128]{1,0:T(8,128)}, u32[]{:S(2)}) copy-start(f32[1024,128]{1,0:T(8,128)} %get-tuple-element.12) | copy-start | bytes 1572868
  181.7 4.7 %copy-start.3 = (bf16[2,2,80,1024]{3,2,1,0:T(8,128)(2,1)S(1)}, bf16[2,2,80,1024]{3,2,1,0:T(8,128)(2,1)}, u32[]{:S(2)}) copy-start(bf16[2,2,80,1024]{3,2,1,0:T(8,128)(2,1)} %get-tuple-element.11) | copy-start | bytes 1966084
  185.0 2.4 %copy-start.2 = (bf16[2,8,90,1024]{3,1,2,0:T(8,128)(2,1)S(1)}, bf16[2,8,90,1024]{3,1,2,0:T(8,128)(2,1)}, u32[]{:S(2)}) copy-start(bf16[2,8,90,1024]{3,1,2,0:T(8,128)(2,1)} %param.14) | copy-start | bytes 8847364
  185.0 2.4 %copy-start.6 = (f32[8]{0:T(128)S(1)}, f32[8]{0:T(128)}, u32[]{:S(2)}) copy-start(f32[8]{0:T(128)} %area_ref.1) | copy-start | bytes 100

commit v2 on v1

--- a/solution.py
+++ b/solution.py
@@ -16,20 +16,15 @@
 NLAT = 16
 NLON = 4
 ROWS = 8
-MAIN = 80
-REST = 10
+COLS = LON // NLON
+AREA = COLS * ROWS
 KL = 11
-WINDOW = 32
 CHUNKS = 8
 HALF = 4
 SPAN = 2 * MODES
 LINES = KL * LAT
 BF = jnp.bfloat16
 F32 = jnp.float32
-
-
-def window_start(h):
-    return min(REST * h // 16 * 16, MAIN - WINDOW)
 
 
 def build_tables():
@@ -41,26 +36,6 @@
     weight = np.where(k == 0, 1.0, 2.0)
     forward = np.concatenate([cos, -sin], axis=1)
     back = np.concatenate([weight * cos, -weight * sin], axis=1)
-
-    def arranged(table):
-        here = table.reshape(NLON, MAIN + REST, SPAN)
-        main = here[:, :MAIN].reshape(NLON * MAIN, SPAN)
-        rest = np.zeros((ROWS, NLON, WINDOW, SPAN))
-        for h in range(ROWS):
-            at = REST * h - window_start(h)
-            rest[h, :, at : at + REST] = here[:, MAIN:]
-        return main, rest.reshape(ROWS, NLON * WINDOW, SPAN)
-
-    first, second, main_out, rest_out = [], [], [], []
-    for there, home in ((forward, back), (back, forward)):
-        main, rest = arranged(there)
-        first.append(main[:256].T)
-        second.append(
-            np.stack([np.concatenate([main[256:], rest[h]], axis=0).T for h in range(ROWS)])
-        )
-        main, rest = arranged(home)
-        main_out.append(main)
-        rest_out.append(rest)
     h = np.arange(LAT)
     angle = (h[:, None] * h[None, :] % LAT).astype(np.float32) * np.float32(2.0 * math.pi / LAT)
     c = np.cos(angle) / math.sqrt(LAT)
@@ -69,10 +44,8 @@
     square = square.reshape(2, NLAT, ROWS, 2, LAT).transpose(1, 0, 2, 3, 4).reshape(256, 256)
     cast = lambda a: np.asarray(a, np.float32).astype(jnp.bfloat16)
     return (
-        cast(np.stack(first)),
-        cast(np.stack(second)),
-        cast(np.stack(main_out)),
-        cast(np.stack(rest_out)),
+        cast(np.stack([forward.T, back.T])),
+        cast(np.stack([back, forward])),
         cast(square.T),
         cast(square),
     )
@@ -87,11 +60,11 @@
 
 
 def kernel(
-    x_ref, g_ref, xr_ref, gr_ref, area_ref, w1_ref, b1_ref, w2_ref, b2_ref,
-    first_hbm, second_hbm, main_hbm, rest_hbm, latf_ref, latb_ref,
-    out_main, out_rest, gw_ref, gb_ref,
-    first, second, main_tab, rest_tab,
-    ybuf, l1s, l1r, l2s, l2r, y2s, tmp, tmp2, racc,
+    x_ref, g_ref, area_ref, w1_ref, b1_ref, w2_ref, b2_ref,
+    lonf_hbm, lonb_hbm, latf_ref, latb_ref,
+    outx_ref, outg_ref, gw1_ref, gw2_ref, gb1_ref, gb2_ref,
+    lonf, lonb,
+    ybuf, l1s, l1r, l2s, l2r, y2s, tmp, tmp2, cells, cells2,
     sa, hs, gps, sls, shb, dbuf1, dbuf2, wc, wt, bias, acc1, acc2, accb,
     gsend, grecv, xs, xr, ag, brows,
     y1_s, y1_r, l1_s, l1_r, l2_s, l2_r, y2_s, y2_r, t_s, g_s, g_r, p_s, p_r, a_s, a_r,
@@ -103,7 +76,7 @@
     tables = [
         pltpu.make_async_copy(src, dst, t_s.at[i])
         for i, (src, dst) in enumerate(
-            ((first_hbm, first), (second_hbm, second), (main_hbm, main_tab), (rest_hbm, rest_tab))
+            ((lonf_hbm, lonf), (lonb_hbm, lonb))
         )
     ]
     for copy in tables:
@@ -129,32 +102,28 @@
         c = lax.rem(t, HALF)
         return c // 2, lax.rem(c, 2)
 
-    def y1_from(t, field, rest):
+    def y1_from(t, field):
         b, n = place(t)
         for i in (2, 1, 3, 0):
             j = lax.rem(col + i, NLON)
             lanes = pl.ds(pl.multiple_of((2 * j + n) * 128, 128), 128)
-            pairs = (
-                (field.at[b, :, pl.ds(0, MAIN), lanes], ybuf.at[t, col, pl.ds(0, ROWS)]),
-                (rest.at[b, :, lanes], ybuf.at[t, col, ROWS]),
-            )
-            for src, dst in pairs:
-                if i:
-                    pltpu.make_async_remote_copy(
-                        src, dst, y1_s.at[t], y1_r.at[t],
-                        device_id={"lon": j}, device_id_type=MESH,
-                    ).start()
-                else:
-                    pltpu.make_async_copy(src, dst, y1_r.at[t]).start()
+            src, dst = field.at[b, :, lanes], ybuf.at[t, col]
+            if i:
+                pltpu.make_async_remote_copy(
+                    src, dst, y1_s.at[t], y1_r.at[t],
+                    device_id={"lon": j}, device_id_type=MESH,
+                ).start()
+            else:
+                pltpu.make_async_copy(src, dst, y1_r.at[t]).start()
 
     def y1_send(t):
         @pl.when(t < HALF)
         def _():
-            y1_from(t, x_ref, xr_ref)
+            y1_from(t, x_ref)
 
         @pl.when(t >= HALF)
         def _():
-            y1_from(t, g_ref, gr_ref)
+            y1_from(t, g_ref)
 
     def wait_bytes(ref, sem):
         pltpu.make_async_copy(ref, ref, sem).wait()
@@ -181,9 +150,6 @@
     for copy in tables:
         copy.wait()
 
-    def rest_window(h):
-        return pl.multiple_of(jnp.minimum(REST * h // 16 * 16, MAIN - WINDOW), 16)
-
     def stage_a(t):
         kind = t // HALF
         slot = lax.rem(t, 2)
@@ -193,16 +159,21 @@
         def _():
             y1_send(t + 2)
 
-        def row(h, _):
-            cols = ybuf[t, :, h].reshape(NLON * MAIN, 128)
-            rest = ybuf[t, :, ROWS, pl.ds(rest_window(h), WINDOW), :].reshape(NLON * WINDOW, 128)
-            tail = jnp.concatenate([cols[256:], rest], axis=0)
-            modes = dot(first[kind], cols[:256]) + dot(second[kind, h], tail)
-            scale = jnp.where(kind == 0, 1.0, area_ref[h])
-            tmp[pl.ds(pl.multiple_of(h * SPAN, 8), SPAN), :] = modes * scale
-            return 0
-
-        lax.fori_loop(0, ROWS, row, 0)
+        for j in range(NLON):
+            cells[j * AREA : (j + 1) * AREA, :] = ybuf[t, j].astype(F32)
+
+        def rows(i, _):
+            h = 2 * i
+            field = jnp.concatenate(
+                [cells[pl.ds(h + q, LON, stride=ROWS), :].astype(BF) for q in range(2)], axis=1
+            )
+            modes = dot(lonf[kind], field)
+            for q in range(2):
+                scale = jnp.where(kind == 0, 1.0, area_ref[h + q])
+                tmp[pl.ds(h + q, SPAN, stride=ROWS), :] = modes[:, q * 128 : (q + 1) * 128] * scale
+            return 0
+
+        lax.fori_loop(0, ROWS // 2, rows, 0)
 
         @pl.when(t >= 2)
         def _():
@@ -210,16 +181,12 @@
 
         def peer(i, _):
             l = lax.rem(me + i, NLAT)
-            for kk in range(KL):
-                k = l * KL + kk
-                tile = jnp.concatenate(
-                    [
-                        tmp[pl.ds(k, ROWS, stride=SPAN), :],
-                        tmp[pl.ds(k + MODES, ROWS, stride=SPAN), :],
-                    ],
-                    axis=0,
-                ).astype(BF)
-                l1s[slot, l, kk] = tile
+            at = pl.multiple_of(l * (KL * ROWS), ROWS)
+            both = [
+                tmp[pl.ds(at + p * (MODES * ROWS), KL * ROWS), :].reshape(KL, ROWS, 128)
+                for p in range(2)
+            ]
+            l1s[slot, l] = jnp.concatenate(both, axis=1).astype(BF)
 
             @pl.when(i > 0)
             def _():
@@ -325,11 +292,11 @@
         wait_bytes(l2r.at[t, pl.ds(0, NLAT - 1)], l2_r.at[t])
 
         def peer(l, _):
-            for kk in range(KL):
-                k = l * KL + kk
-                v = l2r[t, l, kk].astype(F32)
-                tmp2[pl.ds(k, ROWS, stride=SPAN), :] = v[:ROWS]
-                tmp2[pl.ds(k + MODES, ROWS, stride=SPAN), :] = v[ROWS:]
+            v = l2r[t, l].astype(F32)
+            at = pl.multiple_of(l * (KL * ROWS), ROWS)
+            for p in range(2):
+                half = v[:, p * ROWS : (p + 1) * ROWS].reshape(KL * ROWS, 128)
+                tmp2[pl.ds(at + p * (MODES * ROWS), KL * ROWS), :] = half
             return 0
 
         lax.fori_loop(0, NLAT, peer, 0)
@@ -338,26 +305,25 @@
         def _():
             wait_bytes(y2s.at[slot], y2_s.at[t - 2])
 
-        racc[...] = jnp.zeros_like(racc)
-
-        def row(h, _):
-            s = tmp2[pl.ds(pl.multiple_of(h * SPAN, 8), SPAN), :].astype(BF)
-            y2s[slot, :, h] = dot(main_tab[kind], s).astype(BF).reshape(NLON, MAIN, 128)
-            racc[:, pl.ds(rest_window(h), WINDOW), :] += dot(rest_tab[kind, h], s).reshape(
-                NLON, WINDOW, 128
+        def rows(i, _):
+            h = 2 * i
+            modes = jnp.concatenate(
+                [tmp2[pl.ds(h + q, SPAN, stride=ROWS), :].astype(BF) for q in range(2)], axis=1
             )
-            return 0
-
-        lax.fori_loop(0, ROWS, row, 0)
-        y2s[slot, :, ROWS] = racc[...].astype(BF)
+            field = dot(lonb[kind], modes)
+            for q in range(2):
+                cells2[pl.ds(h + q, LON, stride=ROWS), :] = field[:, q * 128 : (q + 1) * 128]
+            return 0
+
+        lax.fori_loop(0, ROWS // 2, rows, 0)
+        for j in range(NLON):
+            y2s[slot, j] = cells2[j * AREA : (j + 1) * AREA, :].astype(BF)
         lanes = pl.ds(pl.multiple_of((2 * col + n) * 128, 128), 128)
-        for i in (2, 1, 3, 0):
-            j = lax.rem(col + i, NLON)
-            pairs = (
-                (y2s.at[slot, j, pl.ds(0, ROWS)], out_main.at[kind, b, :, :, lanes]),
-                (y2s.at[slot, j, ROWS], out_rest.at[kind, b, :, lanes]),
-            )
-            for src, dst in pairs:
+
+        def y2_to(out):
+            for i in (2, 1, 3, 0):
+                j = lax.rem(col + i, NLON)
+                src, dst = y2s.at[slot, j], out.at[b, :, lanes]
                 if i:
                     pltpu.make_async_remote_copy(
                         src, dst, y2_s.at[t], y2_r.at[t],
@@ -365,6 +331,14 @@
                     ).start()
                 else:
                     pltpu.make_async_copy(src, dst, y2_s.at[t]).start()
+
+        @pl.when(kind == 0)
+        def _():
+            y2_to(outx_ref)
+
+        @pl.when(kind == 1)
+        def _():
+            y2_to(outg_ref)
 
     def scatter_grads():
         gsend[...] = jnp.zeros_like(gsend)
@@ -420,8 +394,12 @@
         lax.fori_loop(1, NLAT, peer, 0)
         wait_bytes(ag.at[pl.ds(0, NLAT - 1)], a_r)
         for l in range(NLAT):
-            gw_ref[l * 64 : (l + 1) * 64, :] = ag[l, 0:64].astype(F32)
-        gb_ref[...] = ag[0, 64:80].astype(F32)[:8]
+            out = (gw1_ref, gw2_ref)[l // 8]
+            out[l % 8 // 4, l % 4 // 2, l % 2 * 64 : (l % 2 + 1) * 64, :] = ag[l, 0:64].astype(F32)
+        biases = ag[0, 64:80].astype(F32)
+        for at in range(8):
+            out = (gb1_ref, gb2_ref)[at // 4]
+            out[at % 4 // 2, at % 2 : at % 2 + 1, :] = biases[at : at + 1]
         wait_bytes(ag.at[pl.ds(0, NLAT - 1)], a_s)
         wait_bytes(gsend.at[pl.ds(0, NLAT - 1)], g_s)
 
@@ -467,37 +445,41 @@
 def per_device(inputs, cotangent, area, w1, b1, w2, b2):
     members, rows, cols, channels = inputs.shape
     tables = [jnp.asarray(a) for a in build_tables()]
-    x_rest = inputs[:, :, MAIN:, :].reshape(members, rows * REST, channels)
-    g_rest = cotangent[:, :, MAIN:, :].reshape(members, rows * REST, channels)
+
+    def merged(field):
+        return field.transpose(0, 2, 1, 3).reshape(members, cols * rows, channels)
+
+    x, g = merged(inputs), merged(cotangent)
     anywhere = pl.BlockSpec(memory_space=pl.ANY)
     vmem = pl.BlockSpec(memory_space=pltpu.VMEM)
     smem = pl.BlockSpec(memory_space=pltpu.SMEM)
     dma = pltpu.SemaphoreType.DMA
     V = pltpu.VMEM
-    out_main, out_rest, gw, gb = pl.pallas_call(
+    correction, back, gw1, gw2, gb1, gb2 = pl.pallas_call(
         kernel,
         out_shape=(
-            jax.ShapeDtypeStruct((2, members, rows, MAIN, channels), BF),
-            jax.ShapeDtypeStruct((2, members, rows * REST, channels), BF),
-            jax.ShapeDtypeStruct((1024, 128), F32),
-            jax.ShapeDtypeStruct((8, 128), F32),
+            jax.ShapeDtypeStruct(x.shape, BF),
+            jax.ShapeDtypeStruct(g.shape, BF),
+            jax.ShapeDtypeStruct(w1.shape, F32),
+            jax.ShapeDtypeStruct(w2.shape, F32),
+            jax.ShapeDtypeStruct(b1.shape, F32),
+            jax.ShapeDtypeStruct(b2.shape, F32),
         ),
-        in_specs=[anywhere] * 4 + [smem] + [vmem] * 4 + [anywhere] * 4 + [vmem] * 2,
-        out_specs=(anywhere, anywhere, vmem, vmem),
+        in_specs=[anywhere] * 2 + [smem] + [vmem] * 4 + [anywhere] * 2 + [vmem] * 2,
+        out_specs=(anywhere, anywhere, vmem, vmem, vmem, vmem),
         scratch_shapes=[
-            V((2, SPAN, 256), BF),
-            V((2, ROWS, SPAN, 192), BF),
-            V((2, NLON * MAIN, SPAN), BF),
-            V((2, ROWS, NLON * WINDOW, SPAN), BF),
-            V((CHUNKS, NLON, ROWS + 1, MAIN, 128), BF),
+            V((2, SPAN, LON), BF),
+            V((2, LON, SPAN), BF),
+            V((CHUNKS, NLON, AREA, 128), BF),
             V((2, NLAT, KL, 16, 128), BF),
             V((CHUNKS, NLAT, KL, 16, 128), BF),
             V((2, NLAT, KL, 16, 128), BF),
             V((CHUNKS, NLAT, KL, 16, 128), BF),
-            V((2, NLON, ROWS + 1, MAIN, 128), BF),
+            V((2, NLON, AREA, 128), BF),
             V((ROWS * SPAN, 128), F32),
             V((ROWS * SPAN, 128), F32),
-            V((NLON, MAIN, 128), F32),
+            V((LON * ROWS, 128), F32),
+            V((LON * ROWS, 128), F32),
             V((HALF, LINES, 256), BF),
             V((HALF, LINES, 256), BF),
             V((HALF, LINES, 256), F32),
@@ -519,24 +501,21 @@
             V((16, 128), F32),
         ]
         + [dma((CHUNKS,))] * 8
-        + [dma((4,))]
+        + [dma((2,))]
         + [dma(())] * 6,
         compiler_params=pltpu.CompilerParams(
             collective_id=0, has_side_effects=True, vmem_limit_bytes=60 * 2**20
         ),
         name="afno",
-    )(inputs, cotangent, x_rest, g_rest, area, w1, b1, w2, b2, *tables)
-
-    def whole(kind):
-        rest = out_rest[kind].reshape(members, rows, REST, channels)
-        return jnp.concatenate([out_main[kind], rest], axis=2).astype(F32)
+    )(x, g, area, w1, b1, w2, b2, *tables)
+
+    def split(field):
+        return field.reshape(members, cols, rows, channels).transpose(0, 2, 1, 3).astype(F32)
 
     weighted = (area[None, :, None, None] * cotangent.astype(F32)).astype(BF)
-    output_field = (inputs.astype(F32) + whole(0)).astype(BF)
-    grad_input = (weighted.astype(F32) + whole(1)).astype(BF)
-    gw = gw.reshape(2, 2, 2, 128, 128)
-    gb = gb.reshape(2, 2, 2, 128)
-    return output_field, grad_input, gw[0], gw[1], gb[0], gb[1]
+    output_field = (inputs.astype(F32) + split(correction)).astype(BF)
+    grad_input = (weighted.astype(F32) + split(back)).astype(BF)
+    return output_field, grad_input, gw1, gw2, gb1, gb2
 
 
 def solution(mesh):

time: 203 us -> 181 us (0.89)
  local copies, waits for them, and re-layouts: 23.1 us -> 2.59 us
    unnamed x18 -> x16, local copies, waits for them, and re-layouts: 13.1 us -> 2.59 us
    slice x9 -> x0, local copies, waits for them, and re-layouts: 4.95 us -> none  [the longest x2 1.49 us: per_device(): x_rest = inputs[:, :, MAIN:, :].reshape(members, rows * REST, channels)]
    squeeze x1 -> x0, local copies, waits for them, and re-layouts: 3.27 us -> none  [whole(): return jnp.concatenate([out_main[kind], rest], axis=2).astype(F32)]
where the time goes in v2:
time: 181 us
  Pallas kernels  168 us (93%)
  other arithmetic  9.42 us (5%)
  local copies, waits for them, and re-layouts  2.59 us (1%)
    pallas_call x1, Pallas kernels, per_device(): pl.pallas_call(kernel, out_shape=(jax.ShapeDtypeStruct(x.shape, BF), jax....  168 us
    convert_element_type x1, other arithmetic, per_device(): grad_input = (weighted.astype(F32) + split(back)).astype(BF)  9.42 us

profile of v2, /device:TPU:1, one launch (start us, length us, event | category | flops | bytes accessed | tf_op | source)
XLA Modules:
  0.0 181.2 jit_solution(18009861569646477617)
XLA Ops:
  0.6 0.0 copy-start
  0.6 0.0 copy-start.3
  0.7 168.4 %afno.1 = (bf16[2,720,1024]{2,1,0:T(8,128)(2,1)}, bf16[2,720,1024]{2,1,0:T(8,128)(2,1)}, f32[2,2,128,128]{3,2,1,0:T(8,128)}, f32[2,2,128,128]{3,2,1,0:T(8,128)},...) custom-call(bf16[2,720,1024]{2,1,0:T(8,128)(2,1)} %bitcast.25, bf16[2,720,1024]{2,1,0:T(8,128)(2,1)} %bitcast.24, f32[8]{0:T(128)} %area_ref.1, ...), custom_call_target="tpu_custom_call" | custom-call | tf_op jit(solution)/shard_map/afno/pallas_call | solution.py:458
  169.1 0.0 copy-done
  169.1 0.0 copy-done.3
  169.1 0.0 copy-start.2
  169.1 0.0 copy-start.1
  169.1 0.0 copy-start.5
  169.1 0.0 copy-start.4
  169.2 9.4 %fusion.1 = (bf16[2,8,90,1024]{3,1,2,0:T(8,128)(2,1)}, bf16[2,8,90,1024]{3,1,2,0:T(8,128)(2,1)}) fusion(bf16[2,8,90,1024]{3,1,2,0:T(8,128)(2,1)S(1)} %copy-done, bf16[2,720,1024]{2,1,0:T(8,128)(2,1)} %get-tuple-element.13, f32[8]{0:T(128)S(1)} %copy-done.3, bf16[2,720,1024]{2,1,0:T(8,128)(2,1)} %get-tuple-element.12, bf16[2,8,90,1024]{3,1,2,0:T(8,128)(2,1)} %param.11), kind=kLoop, calls=%fused_computation.2 | loop fusion | flops 16220160 | bytes 17694752 | tf_op jit(solution)/shard_map/convert_element_type | solution.py:517
  178.6 0.0 copy-done.2
  178.6 0.7 copy.21
  179.3 0.0 copy-done.1
  179.3 0.7 copy.22
  180.0 0.0 copy-done.5
  180.0 0.6 copy.23
  180.6 0.0 copy-done.4
  180.6 0.6 copy.24
Async XLA Ops:
  0.6 168.5 %copy-start = (bf16[2,8,90,1024]{3,1,2,0:T(8,128)(2,1)S(1)}, bf16[2,8,90,1024]{3,1,2,0:T(8,128)(2,1)}, u32[]{:S(2)}) copy-start(bf16[2,8,90,1024]{3,1,2,0:T(8,128)(2,1)} %param.12) | copy-start | bytes 8847364
  0.6 168.5 %copy-start.3 = (f32[8]{0:T(128)S(1)}, f32[8]{0:T(128)}, u32[]{:S(2)}) copy-start(f32[8]{0:T(128)} %area_ref.1) | copy-start | bytes 100
  169.1 9.5 %copy-start.2 = (f32[2,2,128,128]{3,2,1,0:T(8,128)S(1)}, f32[2,2,128,128]{3,2,1,0:T(8,128)}, u32[]{:S(2)}) copy-start(f32[2,2,128,128]{3,2,1,0:T(8,128)} %get-tuple-element.28) | copy-start | bytes 786436
  169.1 10.2 %copy-start.1 = (f32[2,2,128,128]{3,2,1,0:T(8,128)S(1)}, f32[2,2,128,128]{3,2,1,0:T(8,128)}, u32[]{:S(2)}) copy-start(f32[2,2,128,128]{3,2,1,0:T(8,128)} %get-tuple-element.29) | copy-start | bytes 786436
  169.1 10.9 %copy-start.5 = (f32[2,2,128]{2,1,0:T(2,128)S(1)}, f32[2,2,128]{2,1,0:T(2,128)}, u32[]{:S(2)}) copy-start(f32[2,2,128]{2,1,0:T(2,128)} %get-tuple-element.30) | copy-start | bytes 6148
  169.1 11.4 %copy-start.4 = (f32[2,2,128]{2,1,0:T(2,128)S(1)}, f32[2,2,128]{2,1,0:T(2,128)}, u32[]{:S(2)}) copy-start(f32[2,2,128]{2,1,0:T(2,128)} %get-tuple-element.31) | copy-start | bytes 6148

commit v3 on v2

--- a/solution.py
+++ b/solution.py
@@ -19,6 +19,7 @@
 COLS = LON // NLON
 AREA = COLS * ROWS
 KL = 11
+LAG_B, LAG_C = 2, 4
 CHUNKS = 8
 HALF = 4
 SPAN = 2 * MODES
@@ -62,7 +63,7 @@
 def kernel(
     x_ref, g_ref, area_ref, w1_ref, b1_ref, w2_ref, b2_ref,
     lonf_hbm, lonb_hbm, latf_ref, latb_ref,
-    outx_ref, outg_ref, gw1_ref, gw2_ref, gb1_ref, gb2_ref,
+    outx_ref, outg_ref, gw_ref, gb_ref,
     lonf, lonb,
     ybuf, l1s, l1r, l2s, l2r, y2s, tmp, tmp2, cells, cells2,
     sa, hs, gps, sls, shb, dbuf1, dbuf2, wc, wt, bias, acc1, acc2, accb,
@@ -394,12 +395,8 @@
         lax.fori_loop(1, NLAT, peer, 0)
         wait_bytes(ag.at[pl.ds(0, NLAT - 1)], a_r)
         for l in range(NLAT):
-            out = (gw1_ref, gw2_ref)[l // 8]
-            out[l % 8 // 4, l % 4 // 2, l % 2 * 64 : (l % 2 + 1) * 64, :] = ag[l, 0:64].astype(F32)
-        biases = ag[0, 64:80].astype(F32)
-        for at in range(8):
-            out = (gb1_ref, gb2_ref)[at // 4]
-            out[at % 4 // 2, at % 2 : at % 2 + 1, :] = biases[at : at + 1]
+            gw_ref[l * 64 : (l + 1) * 64, :] = ag[l, 0:64].astype(F32)
+        gb_ref[...] = ag[0, 64:80].astype(F32)[:8]
         wait_bytes(ag.at[pl.ds(0, NLAT - 1)], a_s)
         wait_bytes(gsend.at[pl.ds(0, NLAT - 1)], g_s)
 
@@ -408,9 +405,9 @@
         def _():
             stage_a(s)
 
-        @pl.when(jnp.logical_and(s >= 1, s <= CHUNKS))
-        def _():
-            t = s - 1
+        @pl.when(jnp.logical_and(s >= LAG_B, s < CHUNKS + LAG_B))
+        def _():
+            t = s - LAG_B
             wait_bytes(l1r.at[t, pl.ds(0, NLAT - 1)], l1_r.at[t])
 
             @pl.when(t < HALF)
@@ -421,17 +418,17 @@
             def _():
                 stage_b_backward(t)
 
-        @pl.when(s == CHUNKS)
+        @pl.when(s == CHUNKS + LAG_B - 1)
         def _():
             scatter_grads()
 
-        @pl.when(s >= 2)
-        def _():
-            stage_c(s - 2)
+        @pl.when(s >= LAG_C)
+        def _():
+            stage_c(s - LAG_C)
 
         return 0
 
-    lax.fori_loop(0, CHUNKS + 2, slot_of, 0)
+    lax.fori_loop(0, CHUNKS + LAG_C, slot_of, 0)
     finish_grads()
     for t in range(CHUNKS):
         wait_bytes(ybuf.at[t, pl.ds(0, NLON - 1)], y1_s.at[t])
@@ -442,6 +439,18 @@
         wait_bytes(y2s.at[t % 2], y2_s.at[t])
 
 
+def add_kernel(area_ref, x_ref, correction_ref, g_ref, back_ref, field_ref, grad_ref):
+    _, rows, channels = x_ref.shape
+    field_ref[0] = (x_ref[0].astype(F32) + correction_ref[0].astype(F32)).astype(BF)
+    h = lax.broadcasted_iota(jnp.int32, (ROWS, channels), 0)
+    scale = jnp.zeros((ROWS, channels), F32)
+    for q in range(ROWS):
+        scale = jnp.where(h == q, area_ref[q], scale)
+    g = g_ref[0].astype(F32).reshape(rows // ROWS, ROWS, channels)
+    weighted = (g * scale).astype(BF).astype(F32).reshape(rows, channels)
+    grad_ref[0] = (weighted + back_ref[0].astype(F32)).astype(BF)
+
+
 def per_device(inputs, cotangent, area, w1, b1, w2, b2):
     members, rows, cols, channels = inputs.shape
     tables = [jnp.asarray(a) for a in build_tables()]
@@ -455,18 +464,16 @@
     smem = pl.BlockSpec(memory_space=pltpu.SMEM)
     dma = pltpu.SemaphoreType.DMA
     V = pltpu.VMEM
-    correction, back, gw1, gw2, gb1, gb2 = pl.pallas_call(
+    correction, back, gw, gb = pl.pallas_call(
         kernel,
         out_shape=(
             jax.ShapeDtypeStruct(x.shape, BF),
             jax.ShapeDtypeStruct(g.shape, BF),
-            jax.ShapeDtypeStruct(w1.shape, F32),
-            jax.ShapeDtypeStruct(w2.shape, F32),
-            jax.ShapeDtypeStruct(b1.shape, F32),
-            jax.ShapeDtypeStruct(b2.shape, F32),
+            jax.ShapeDtypeStruct((1024, 128), F32),
+            jax.ShapeDtypeStruct((8, 128), F32),
         ),
         in_specs=[anywhere] * 2 + [smem] + [vmem] * 4 + [anywhere] * 2 + [vmem] * 2,
-        out_specs=(anywhere, anywhere, vmem, vmem, vmem, vmem),
+        out_specs=(anywhere, anywhere, vmem, vmem),
         scratch_shapes=[
             V((2, SPAN, LON), BF),
             V((2, LON, SPAN), BF),
@@ -509,13 +516,23 @@
         name="afno",
     )(x, g, area, w1, b1, w2, b2, *tables)
 
+    block = pl.BlockSpec((1, AREA // 5, channels), lambda i, j: (i, j, 0))
+    output_field, grad_input = pl.pallas_call(
+        add_kernel,
+        grid=(members, 5),
+        out_shape=(jax.ShapeDtypeStruct(x.shape, BF), jax.ShapeDtypeStruct(g.shape, BF)),
+        in_specs=[smem] + [block] * 4,
+        out_specs=(block, block),
+        compiler_params=pltpu.CompilerParams(vmem_limit_bytes=60 * 2**20),
+        name="adds",
+    )(area, x, correction, g, back)
+
     def split(field):
-        return field.reshape(members, cols, rows, channels).transpose(0, 2, 1, 3).astype(F32)
-
-    weighted = (area[None, :, None, None] * cotangent.astype(F32)).astype(BF)
-    output_field = (inputs.astype(F32) + split(correction)).astype(BF)
-    grad_input = (weighted.astype(F32) + split(back)).astype(BF)
-    return output_field, grad_input, gw1, gw2, gb1, gb2
+        return field.reshape(members, cols, rows, channels).transpose(0, 2, 1, 3)
+
+    gw = gw.reshape(2, 2, 2, 128, 128)
+    gb = gb.reshape(2, 2, 2, 128)
+    return split(output_field), split(grad_input), gw[0], gw[1], gb[0], gb[1]
 
 
 def solution(mesh):

time: 181 us -> 175 us (0.967)
  other arithmetic: 9.42 us -> 0 us
  Pallas kernels: 168 us -> 172 us
    pallas_call x0 -> x1, Pallas kernels: none -> 9.87 us  [per_device(): pl.pallas_call(add_kernel, grid=(members, 5), out_shape=(jax.ShapeDtypeSt...]
    convert_element_type x1 -> x0, other arithmetic: 9.42 us -> none  [per_device(): grad_input = (weighted.astype(F32) + split(back)).astype(BF)]
    pallas_call x1, Pallas kernels: 168 us -> 162 us  [per_device(): pl.pallas_call(kernel, out_shape=(jax.ShapeDtypeStruct(x.shape, BF), jax....]
    unnamed x16 -> x4, local copies, waits for them, and re-layouts: 2.59 us -> 0.01 us
where the time goes in v3:
time: 175 us; the launch traced here: 174 us
  Pallas kernels  172 us (98%)
    pallas_call x1, Pallas kernels, per_device(): pl.pallas_call(kernel, out_shape=(jax.ShapeDtypeStruct(x.shape, BF), jax....  162 us
    pallas_call x1, Pallas kernels, per_device(): pl.pallas_call(add_kernel, grid=(members, 5), out_shape=(jax.ShapeDtypeSt...  9.87 us

profile of v3, /device:TPU:1, one launch (start us, length us, event | category | flops | bytes accessed | tf_op | source)
XLA Modules:
  0.0 174.4 jit_solution(713622576000124803)
XLA Ops:
  0.6 162.5 %afno.1 = (bf16[2,720,1024]{2,1,0:T(8,128)(2,1)}, bf16[2,720,1024]{2,1,0:T(8,128)(2,1)}, f32[1024,128]{1,0:T(8,128)}, f32[8,128]{1,0:T(8,128)}) custom-call(bf16[2,720,1024]{2,1,0:T(8,128)(2,1)} %bitcast.16, bf16[2,720,1024]{2,1,0:T(8,128)(2,1)} %bitcast.18, f32[8]{0:T(128)} %area_ref.3, bf16[2,2,128,128]{3,2,1,0:T(8,128)(2,1)} %w1_ref.1, ...), custom_call_target="tpu_custom_call" | custom-call | tf_op jit(solution)/shard_map/afno/pallas_call | solution.py:467
  163.1 0.0 copy-start.1
  163.1 0.0 copy-start
  163.1 9.9 %adds.1 = (bf16[2,720,1024]{2,1,0:T(8,128)(2,1)}, bf16[2,720,1024]{2,1,0:T(8,128)(2,1)}) custom-call(f32[8]{0:T(128)} %area_ref.3, bf16[2,720,1024]{2,1,0:T(8,128)(2,1)} %bitcast.17, bf16[2,720,1024]{2,1,0:T(8,128)(2,1)} %get-tuple-element.12.correction_ref, bf16[2,720,1024]{2,1,0:T(8,128)(2,1)} %bitcast.19, bf16[2,720,1024]{2,1,0:T(8,128)(2,1)} %get-tuple-element.13.back_ref), custom_call_target="tpu_custom_call" | custom-call | tf_op jit(solution)/shard_map/adds/pallas_call | solution.py:520
  173.0 0.0 copy-done.1
  173.0 0.6 fusion.1
  173.6 0.0 copy-done
  173.6 0.8 fusion
Async XLA Ops:
  163.1 9.9 %copy-start.1 = (f32[8,128]{1,0:T(8,128)S(1)}, f32[8,128]{1,0:T(8,128)}, u32[]{:S(2)}) copy-start(f32[8,128]{1,0:T(8,128)} %get-tuple-element.17) | copy-start | bytes 12292
  163.1 10.5 %copy-start = (f32[1024,128]{1,0:T(8,128)S(1)}, f32[1024,128]{1,0:T(8,128)}, u32[]{:S(2)}) copy-start(f32[1024,128]{1,0:T(8,128)} %get-tuple-element.16) | copy-start | bytes 1572868

commit v4 on v3

--- a/solution.py
+++ b/solution.py
@@ -65,7 +65,7 @@
     lonf_hbm, lonb_hbm, latf_ref, latb_ref,
     outx_ref, outg_ref, gw_ref, gb_ref,
     lonf, lonb,
-    ybuf, l1s, l1r, l2s, l2r, y2s, tmp, tmp2, cells, cells2,
+    ybuf, l1s, l1r, l2s, l2r, y2s, tmp, cells,
     sa, hs, gps, sls, shb, dbuf1, dbuf2, wc, wt, bias, acc1, acc2, accb,
     gsend, grecv, xs, xr, ag, brows,
     y1_s, y1_r, l1_s, l1_r, l2_s, l2_r, y2_s, y2_r, t_s, g_s, g_r, p_s, p_r, a_s, a_r,
@@ -254,10 +254,10 @@
             half = 0.5 + 0.5 * th
             hid = (u * half).astype(BF)
             hs[t, rows] = hid
-            gps[t, rows] = half + (0.5 * u) * (1.0 - th * th) * (C0 + (3.0 * C1) * sq)
+            gps[t, rows] = (half + (0.5 * u) * (1.0 - th * th) * (C0 + (3.0 * C1) * sq)).astype(BF)
             o = dot(hid, wc[1, n]) + bias[1, n]
             slope = jnp.tanh(o * 4.0)
-            sls[t, rows] = slope * slope
+            sls[t, rows] = (slope * slope).astype(BF)
             shb[rows] = (o - 0.25 * slope).astype(BF)
             return 0
 
@@ -272,9 +272,9 @@
 
         def one(i, _):
             rows = pl.ds(pl.multiple_of(i * BLOCK, 16), BLOCK)
-            d = (dbuf2[rows].astype(F32) * sls[c, rows]).astype(BF)
+            d = (dbuf2[rows].astype(F32) * sls[c, rows].astype(F32)).astype(BF)
             dbuf2[rows] = d
-            dp = (dot(d, wt[1, n]) * gps[c, rows]).astype(BF)
+            dp = (dot(d, wt[1, n]) * gps[c, rows].astype(F32)).astype(BF)
             dbuf1[rows] = dp
             shb[rows] = dot(dp, wt[0, n]).astype(BF)
             accb[n, 0] += jnp.sum(dp.astype(F32), axis=0, keepdims=True)
@@ -297,7 +297,7 @@
             at = pl.multiple_of(l * (KL * ROWS), ROWS)
             for p in range(2):
                 half = v[:, p * ROWS : (p + 1) * ROWS].reshape(KL * ROWS, 128)
-                tmp2[pl.ds(at + p * (MODES * ROWS), KL * ROWS), :] = half
+                tmp[pl.ds(at + p * (MODES * ROWS), KL * ROWS), :] = half
             return 0
 
         lax.fori_loop(0, NLAT, peer, 0)
@@ -309,16 +309,16 @@
         def rows(i, _):
             h = 2 * i
             modes = jnp.concatenate(
-                [tmp2[pl.ds(h + q, SPAN, stride=ROWS), :].astype(BF) for q in range(2)], axis=1
+                [tmp[pl.ds(h + q, SPAN, stride=ROWS), :].astype(BF) for q in range(2)], axis=1
             )
             field = dot(lonb[kind], modes)
             for q in range(2):
-                cells2[pl.ds(h + q, LON, stride=ROWS), :] = field[:, q * 128 : (q + 1) * 128]
+                cells[pl.ds(h + q, LON, stride=ROWS), :] = field[:, q * 128 : (q + 1) * 128]
             return 0
 
         lax.fori_loop(0, ROWS // 2, rows, 0)
         for j in range(NLON):
-            y2s[slot, j] = cells2[j * AREA : (j + 1) * AREA, :].astype(BF)
+            y2s[slot, j] = cells[j * AREA : (j + 1) * AREA, :].astype(BF)
         lanes = pl.ds(pl.multiple_of((2 * col + n) * 128, 128), 128)
 
         def y2_to(out):
@@ -484,13 +484,11 @@
             V((CHUNKS, NLAT, KL, 16, 128), BF),
             V((2, NLON, AREA, 128), BF),
             V((ROWS * SPAN, 128), F32),
-            V((ROWS * SPAN, 128), F32),
-            V((LON * ROWS, 128), F32),
             V((LON * ROWS, 128), F32),
             V((HALF, LINES, 256), BF),
             V((HALF, LINES, 256), BF),
-            V((HALF, LINES, 256), F32),
-            V((HALF, LINES, 256), F32),
+            V((HALF, LINES, 256), BF),
+            V((HALF, LINES, 256), BF),
             V((LINES, 256), BF),
             V((LINES, 256), BF),
             V((LINES, 256), BF),
@@ -511,7 +509,7 @@
         + [dma((2,))]
         + [dma(())] * 6,
         compiler_params=pltpu.CompilerParams(
-            collective_id=0, has_side_effects=True, vmem_limit_bytes=60 * 2**20
+            collective_id=0, has_side_effects=True, vmem_limit_bytes=44 * 2**20
         ),
         name="afno",
     )(x, g, area, w1, b1, w2, b2, *tables)
@@ -523,7 +521,7 @@
         out_shape=(jax.ShapeDtypeStruct(x.shape, BF), jax.ShapeDtypeStruct(g.shape, BF)),
         in_specs=[smem] + [block] * 4,
         out_specs=(block, block),
-        compiler_params=pltpu.CompilerParams(vmem_limit_bytes=60 * 2**20),
+        compiler_params=pltpu.CompilerParams(vmem_limit_bytes=24 * 2**20),
         name="adds",
     )(area, x, correction, g, back)
 

time: 175 us -> 177 us (1.011)
  local copies, waits for them, and re-layouts: 1.42 us -> 9.14 us
  Pallas kernels: 172 us -> 166 us
    unnamed x4 -> x22, local copies, waits for them, and re-layouts: 0.01 us -> 7.73 us
    pallas_call x1, Pallas kernels: 9.87 us -> 5.4 us  [per_device(): pl.pallas_call(add_kernel, grid=(members, 5), out_shape=(jax.ShapeDtypeSt...]
where the time goes in v4:
time: 177 us; the launch traced here: 176 us
  Pallas kernels  166 us (94%)
  local copies, waits for them, and re-layouts  9.14 us (5%)
    pallas_call x1, Pallas kernels, per_device(): pl.pallas_call(kernel, out_shape=(jax.ShapeDtypeStruct(x.shape, BF), jax....  161 us
    unnamed x22, local copies, waits for them, and re-layouts  7.73 us
    pallas_call x1, Pallas kernels, per_device(): pl.pallas_call(add_kernel, grid=(members, 5), out_shape=(jax.ShapeDtypeSt...  5.4 us

profile of v4, /device:TPU:1, one launch (start us, length us, event | category | flops | bytes accessed | tf_op | source)
XLA Modules:
  0.0 176.2 jit_solution(4612589085540482248)
XLA Ops:
  0.6 0.0 copy-start.2
  0.6 1.0 copy-done.2
  1.7 0.0 copy-start.3
  1.7 1.0 copy-done.3
  2.7 0.0 copy-start.4
  2.7 0.9 copy-done.4
  3.6 0.0 copy-start.5
  3.6 0.9 copy-done.5
  4.5 0.0 copy-start.6
  4.5 0.9 copy-done.6
  5.5 0.0 copy-start.7
  5.5 0.9 copy-done.7
  6.4 0.0 copy-start.8
  6.4 0.7 copy-done.8
  7.0 0.0 copy-start.9
  7.0 0.7 copy-done.9
  7.7 0.0 copy-start.10
  7.7 0.7 copy-done.10
  8.4 0.0 copy-start
  8.4 0.0 copy-start.1
  8.4 161.0 %afno.1 = (bf16[2,720,1024]{2,1,0:T(8,128)(2,1)S(1)}, bf16[2,720,1024]{2,1,0:T(8,128)(2,1)S(1)}, f32[1024,128]{1,0:T(8,128)S(1)}, f32[8,128]{1,0:T(8,128)S(1)}) custom-call(bf16[2,720,1024]{2,1,0:T(8,128)(2,1)} %bitcast.16, bf16[2,720,1024]{2,1,0:T(8,128)(2,1)} %bitcast.18, f32[8]{0:T(128)S(1)} %copy-done.8, bf16[2,2,128,128]{3,2,1,0:T(8,128)(2,1)S(1)} %copy-done.4, ...), custom_call_target="tpu_custom_call" | custom-call | tf_op jit(solution)/shard_map/afno/pallas_call | solution.py:467
  169.4 0.0 copy-done
  169.4 0.0 copy-done.1
  169.4 5.4 %adds.1 = (bf16[2,720,1024]{2,1,0:T(8,128)(2,1)}, bf16[2,720,1024]{2,1,0:T(8,128)(2,1)}) custom-call(f32[8]{0:T(128)S(1)} %copy-done.8, bf16[2,720,1024]{2,1,0:T(8,128)(2,1)S(1)} %bitcast.17, bf16[2,720,1024]{2,1,0:T(8,128)(2,1)S(1)} %get-tuple-element.12.correction_ref, bf16[2,720,1024]{2,1,0:T(8,128)(2,1)S(1)} %bitcast.19, ...), custom_call_target="tpu_custom_call" | custom-call | tf_op jit(solution)/shard_map/adds/pallas_call | solution.py:518
  174.8 0.6 fusion.1
  175.4 0.8 fusion
Async XLA Ops:
  0.6 1.1 copy-start.2
  1.7 1.0 copy-start.3
  2.7 0.9 copy-start.4
  3.6 0.9 copy-start.5
  4.5 0.9 copy-start.6
  5.5 0.9 copy-start.7
  6.4 0.7 copy-start.8
  7.0 0.7 copy-start.9
  7.7 0.7 copy-start.10
  8.4 161.0 %copy-start = (bf16[2,8,90,1024]{3,1,2,0:T(8,128)(2,1)S(1)}, bf16[2,8,90,1024]{3,1,2,0:T(8,128)(2,1)}, u32[]{:S(2)}) copy-start(bf16[2,8,90,1024]{3,1,2,0:T(8,128)(2,1)} %param.11) | copy-start | bytes 8847364
  8.4 161.0 %copy-start.1 = (bf16[2,8,90,1024]{3,1,2,0:T(8,128)(2,1)S(1)}, bf16[2,8,90,1024]{3,1,2,0:T(8,128)(2,1)}, u32[]{:S(2)}) copy-start(bf16[2,8,90,1024]{3,1,2,0:T(8,128)(2,1)} %param.12) | copy-start | bytes 8847364

commit v5 on v4

--- a/solution.py
+++ b/solution.py
@@ -24,6 +24,10 @@
 HALF = 4
 SPAN = 2 * MODES
 LINES = KL * LAT
+LON_PAD = 368
+BACK_AT = 2 * SPAN
+LATF_AT = BACK_AT + 2 * LON_PAD
+LATB_AT = LATF_AT + 256
 BF = jnp.bfloat16
 F32 = jnp.float32
 
@@ -43,13 +47,14 @@
     s = np.sin(angle) / math.sqrt(LAT)
     square = np.stack([np.stack([c, -s], axis=1), np.stack([s, c], axis=1)], axis=0)
     square = square.reshape(2, NLAT, ROWS, 2, LAT).transpose(1, 0, 2, 3, 4).reshape(256, 256)
-    cast = lambda a: np.asarray(a, np.float32).astype(jnp.bfloat16)
-    return (
-        cast(np.stack([forward.T, back.T])),
-        cast(np.stack([back, forward])),
-        cast(square.T),
-        cast(square),
-    )
+    table = np.zeros((LATB_AT + 256, 384), np.float32)
+    for kind, (there, home) in enumerate(((forward, back), (back, forward))):
+        table[kind * SPAN : (kind + 1) * SPAN, :LON] = there.T
+        at = BACK_AT + kind * LON_PAD
+        table[at : at + LON, :SPAN] = home
+    table[LATF_AT : LATF_AT + 256, :256] = square.T
+    table[LATB_AT : LATB_AT + 256, :256] = square
+    return table.astype(jnp.bfloat16)
 
 
 def dot(a, b):
@@ -62,26 +67,16 @@
 
 def kernel(
     x_ref, g_ref, area_ref, w1_ref, b1_ref, w2_ref, b2_ref,
-    lonf_hbm, lonb_hbm, latf_ref, latb_ref,
+    tab_ref,
     outx_ref, outg_ref, gw_ref, gb_ref,
-    lonf, lonb,
     ybuf, l1s, l1r, l2s, l2r, y2s, tmp, cells,
     sa, hs, gps, sls, shb, dbuf1, dbuf2, wc, wt, bias, acc1, acc2, accb,
     gsend, grecv, xs, xr, ag, brows,
-    y1_s, y1_r, l1_s, l1_r, l2_s, l2_r, y2_s, y2_r, t_s, g_s, g_r, p_s, p_r, a_s, a_r,
+    y1_s, y1_r, l1_s, l1_r, l2_s, l2_r, y2_s, y2_r, g_s, g_r, p_s, p_r, a_s, a_r,
 ):
     me = lax.axis_index("lat")
     col = lax.axis_index("lon")
     member = lax.axis_index("batch")
-
-    tables = [
-        pltpu.make_async_copy(src, dst, t_s.at[i])
-        for i, (src, dst) in enumerate(
-            ((lonf_hbm, lonf), (lonb_hbm, lonb))
-        )
-    ]
-    for copy in tables:
-        copy.start()
 
     barrier = pltpu.get_barrier_semaphore()
 
@@ -148,8 +143,6 @@
     acc1[...] = jnp.zeros_like(acc1)
     acc2[...] = jnp.zeros_like(acc2)
     accb[...] = jnp.zeros_like(accb)
-    for copy in tables:
-        copy.wait()
 
     def stage_a(t):
         kind = t // HALF
@@ -168,7 +161,8 @@
             field = jnp.concatenate(
                 [cells[pl.ds(h + q, LON, stride=ROWS), :].astype(BF) for q in range(2)], axis=1
             )
-            modes = dot(lonf[kind], field)
+            at = pl.multiple_of(kind * SPAN, 16)
+            modes = dot(tab_ref[pl.ds(at, SPAN), :LON], field)
             for q in range(2):
                 scale = jnp.where(kind == 0, 1.0, area_ref[h + q])
                 tmp[pl.ds(h + q, SPAN, stride=ROWS), :] = modes[:, q * 128 : (q + 1) * 128] * scale
@@ -204,7 +198,7 @@
     def lat_forward(t, out, at):
         def one(k, _):
             z = l1r[t, :, k].reshape(256, 128)
-            sp = dot(latf_ref[...], z).astype(BF)
+            sp = dot(tab_ref[LATF_AT : LATF_AT + 256, :256], z).astype(BF)
             rows = pl.ds(pl.multiple_of(k * LAT, LAT), LAT)
             view = out.at[at] if at is not None else out
             view[rows, 0:128] = sp[:128]
@@ -221,7 +215,7 @@
         def one(k, _):
             rows = pl.ds(pl.multiple_of(k * LAT, LAT), LAT)
             s = jnp.concatenate([shb[rows, 0:128], shb[rows, 128:256]], axis=0)
-            l2s[slot, :, k] = dot(latb_ref[...], s).astype(BF).reshape(NLAT, 16, 128)
+            l2s[slot, :, k] = dot(tab_ref[LATB_AT : LATB_AT + 256, :256], s).astype(BF).reshape(NLAT, 16, 128)
             return 0
 
         lax.fori_loop(0, KL, one, 0)
@@ -311,7 +305,8 @@
             modes = jnp.concatenate(
                 [tmp[pl.ds(h + q, SPAN, stride=ROWS), :].astype(BF) for q in range(2)], axis=1
             )
-            field = dot(lonb[kind], modes)
+            at = pl.multiple_of(BACK_AT + kind * LON_PAD, 16)
+            field = dot(tab_ref[pl.ds(at, LON_PAD), :SPAN], modes)[:LON]
             for q in range(2):
                 cells[pl.ds(h + q, LON, stride=ROWS), :] = field[:, q * 128 : (q + 1) * 128]
             return 0
@@ -453,7 +448,7 @@
 
 def per_device(inputs, cotangent, area, w1, b1, w2, b2):
     members, rows, cols, channels = inputs.shape
-    tables = [jnp.asarray(a) for a in build_tables()]
+    table = jnp.asarray(build_tables())
 
     def merged(field):
         return field.transpose(0, 2, 1, 3).reshape(members, cols * rows, channels)
@@ -472,11 +467,9 @@
             jax.ShapeDtypeStruct((1024, 128), F32),
             jax.ShapeDtypeStruct((8, 128), F32),
         ),
-        in_specs=[anywhere] * 2 + [smem] + [vmem] * 4 + [anywhere] * 2 + [vmem] * 2,
+        in_specs=[anywhere] * 2 + [smem] + [vmem] * 5,
         out_specs=(anywhere, anywhere, vmem, vmem),
         scratch_shapes=[
-            V((2, SPAN, LON), BF),
-            V((2, LON, SPAN), BF),
             V((CHUNKS, NLON, AREA, 128), BF),
             V((2, NLAT, KL, 16, 128), BF),
             V((CHUNKS, NLAT, KL, 16, 128), BF),
@@ -506,13 +499,12 @@
             V((16, 128), F32),
         ]
         + [dma((CHUNKS,))] * 8
-        + [dma((2,))]
         + [dma(())] * 6,
         compiler_params=pltpu.CompilerParams(
             collective_id=0, has_side_effects=True, vmem_limit_bytes=44 * 2**20
         ),
         name="afno",
-    )(x, g, area, w1, b1, w2, b2, *tables)
+    )(x, g, area, w1, b1, w2, b2, table)
 
     block = pl.BlockSpec((1, AREA // 5, channels), lambda i, j: (i, j, 0))
     output_field, grad_input = pl.pallas_call(

time: 177 us -> 174 us (0.983)
  local copies, waits for them, and re-layouts: 9.14 us -> 6.61 us
    unnamed x22 -> x16, local copies, waits for them, and re-layouts: 7.73 us -> 5.2 us
where the time goes in v5:
time: 174 us
  Pallas kernels  166 us (95%)
  local copies, waits for them, and re-layouts  6.61 us (4%)
    pallas_call x1, Pallas kernels, per_device(): pl.pallas_call(kernel, out_shape=(jax.ShapeDtypeStruct(x.shape, BF), jax....  161 us
    pallas_call x1, Pallas kernels, per_device(): pl.pallas_call(add_kernel, grid=(members, 5), out_shape=(jax.ShapeDtypeSt...  5.4 us
    unnamed x16, local copies, waits for them, and re-layouts  5.2 us

profile of v5, /device:TPU:1, one launch (start us, length us, event | category | flops | bytes accessed | tf_op | source)
XLA Modules:
  0.0 173.5 jit_solution(14516613706149072140)
XLA Ops:
  0.6 0.0 copy-start.2
  0.6 1.4 copy-done.2
  2.0 0.0 copy-start.3
  2.0 0.9 copy-done.3
  2.9 0.0 copy-start.4
  2.9 0.9 copy-done.4
  3.8 0.0 copy-start.5
  3.8 0.7 copy-done.5
  4.5 0.0 copy-start.6
  4.5 0.7 copy-done.6
  5.2 0.0 copy-start.7
  5.2 0.7 copy-done.7
  5.8 0.0 copy-start
  5.8 0.0 copy-start.1
  5.8 160.8 %afno.1 = (bf16[2,720,1024]{2,1,0:T(8,128)(2,1)S(1)}, bf16[2,720,1024]{2,1,0:T(8,128)(2,1)S(1)}, f32[1024,128]{1,0:T(8,128)S(1)}, f32[8,128]{1,0:T(8,128)S(1)}) custom-call(bf16[2,720,1024]{2,1,0:T(8,128)(2,1)} %bitcast.16, bf16[2,720,1024]{2,1,0:T(8,128)(2,1)} %bitcast.18, f32[8]{0:T(128)S(1)} %copy-done.5, bf16[2,2,128,128]{3,2,1,0:T(8,128)(2,1)S(1)} %copy-done.3, ...), custom_call_target="tpu_custom_call" | custom-call | tf_op jit(solution)/shard_map/afno/pallas_call | solution.py:462
  166.7 0.0 copy-done
  166.7 0.0 copy-done.1
  166.7 5.4 %adds.1 = (bf16[2,720,1024]{2,1,0:T(8,128)(2,1)}, bf16[2,720,1024]{2,1,0:T(8,128)(2,1)}) custom-call(f32[8]{0:T(128)S(1)} %copy-done.5, bf16[2,720,1024]{2,1,0:T(8,128)(2,1)S(1)} %bitcast.17, bf16[2,720,1024]{2,1,0:T(8,128)(2,1)S(1)} %get-tuple-element.12.correction_ref, bf16[2,720,1024]{2,1,0:T(8,128)(2,1)S(1)} %bitcast.19, ...), custom_call_target="tpu_custom_call" | custom-call | tf_op jit(solution)/shard_map/adds/pallas_call | solution.py:510
  172.1 0.6 fusion.1
  172.7 0.8 fusion
Async XLA Ops:
  0.6 1.4 copy-start.2
  2.0 0.9 copy-start.3
  2.9 0.9 copy-start.4
  3.8 0.7 copy-start.5
  4.5 0.7 copy-start.6
  5.2 0.7 copy-start.7
  5.8 160.8 %copy-start = (bf16[2,8,90,1024]{3,1,2,0:T(8,128)(2,1)S(1)}, bf16[2,8,90,1024]{3,1,2,0:T(8,128)(2,1)}, u32[]{:S(2)}) copy-start(bf16[2,8,90,1024]{3,1,2,0:T(8,128)(2,1)} %param.8) | copy-start | bytes 8847364
  5.8 160.8 %copy-start.1 = (bf16[2,8,90,1024]{3,1,2,0:T(8,128)(2,1)S(1)}, bf16[2,8,90,1024]{3,1,2,0:T(8,128)(2,1)}, u32[]{:S(2)}) copy-start(bf16[2,8,90,1024]{3,1,2,0:T(8,128)(2,1)} %param.9) | copy-start | bytes 8847364
